TPU v7x, 256 devices: a whole 4x4x8 slice. The times are simulated.
256 devices in a mesh: dp: 8 (over x, y_lo), mp: 32 (over y_hi, z, core).
Axes of the slice: x: 4, y: 4 (y_hi: 2, y_lo: 2; y = y_hi * 2 + y_lo), z: 8, core: 2. Of those that a mesh axis runs over, the one named last changes fastest.
Arguments:
- tokens: bfloat16 [2048, 4096], P('dp', 'mp'), may hold values from -6 to 6
- cotangent: bfloat16 [2048, 4096], P('dp', 'mp'), may hold values from -6 to 6
- gate_weight: bfloat16 [4096, 16384], P('dp', 'mp'), may hold values from -0.1875 to 0.1875
- up_weight: bfloat16 [4096, 16384], P('dp', 'mp'), may hold values from -0.1875 to 0.1875
- down_weight: bfloat16 [16384, 4096], P('mp', 'dp'), may hold values from -0.09375 to 0.09375
- gate_mask: int32 [32, 128], P('dp', 'mp'), may hold values from 0 to 1, as said below
- up_mask: int32 [32, 128], P('dp', 'mp'), may hold values from 0 to 1, as said below
- down_mask: int32 [128, 32], P('mp', 'dp'), may hold values from 0 to 1, as said below
Outputs:
- layer_out: bfloat16 [2048, 4096], P('dp', 'mp')
- token_grad: bfloat16 [2048, 4096], P('dp', 'mp')
- gate_grad: bfloat16 [4096, 16384], P('dp', 'mp')
- up_grad: bfloat16 [4096, 16384], P('dp', 'mp')
- down_grad: bfloat16 [16384, 4096], P('mp', 'dp')
Inputs may be any that keep to these rules, and one draw needn't show every extreme that they name: `gate_mask`: each device's part of the mask (4 x 4 blocks) has 1 to 8 nonzero blocks; in every draw all parts of one index of mp, chosen by the seed, have exactly 8, the same index for the three masks. `up_mask`: each device's part of the mask (4 x 4 blocks) has 1 to 8 nonzero blocks; in every draw all parts of one index of mp, chosen by the seed, have exactly 8, the same index for the three masks. `down_mask`: each device's part of the mask (4 x 4 blocks) has 1 to 8 nonzero blocks; in every draw all parts of one index of mp, chosen by the seed, have exactly 8, the same index for the three masks.
All inputs are finite; a program needn't handle non-finite values.
Results may differ from a plain program's by a relative error of at most 0.017.
Values may be sent and summed in bfloat16 or wider, within the bound.
A program may use at most 128 MiB of HBM per device.

v0:
```python
import math

import jax
import jax.numpy as jnp
from jax import lax
from jax.sharding import PartitionSpec as P

BLK = 128


def to_tiles(matrix, tile_size):
    row_count = matrix.shape[0] // tile_size
    col_count = matrix.shape[1] // tile_size
    shaped = matrix.reshape(row_count, tile_size, col_count, tile_size).transpose(0, 2, 1, 3)
    return shaped.reshape(row_count * col_count, tile_size * tile_size)


def from_tiles(tile_rows, row_count, col_count, tile_size):
    shaped = tile_rows.reshape(row_count, col_count, tile_size, tile_size).transpose(0, 2, 1, 3)
    return shaped.reshape(row_count * tile_size, col_count * tile_size)


def body(tokens, cotangent, gate_weight, up_weight, down_weight, gate_mask, up_mask, down_mask):
    tile_size = BLK
    local_rows = tokens.shape[0]
    dp_count = lax.axis_size("dp")
    full_tokens, full_cotangent = (
        lax.all_gather(tokens, "mp", axis=1, tiled=True),
        lax.all_gather(cotangent, "mp", axis=1, tiled=True),
    )
    row_tiles = gate_weight.shape[0] // tile_size
    col_tiles = gate_weight.shape[1] // tile_size
    tile_count = row_tiles * col_tiles
    capacity = tile_count // 2
    shards = [gate_weight, up_weight, down_weight.T]
    mask_table = jnp.stack(
        [
            gate_mask.reshape(tile_count),
            up_mask.reshape(tile_count),
            down_mask.T.reshape(tile_count),
        ]
    )
    slot_of = jnp.cumsum(mask_table, axis=1) - 1
    own_slot = jnp.where(mask_table > 0, slot_of, 0)
    slot_hits = (slot_of[:, None, :] == jnp.arange(capacity, dtype=jnp.int32)[None, :, None]) & (
        mask_table[:, None, :] > 0
    )
    tile_index = jnp.arange(tile_count, dtype=jnp.int32)
    own_ids = jnp.where(
        jnp.any(slot_hits, axis=2),
        jnp.sum(jnp.where(slot_hits, tile_index[None, None, :], 0), axis=2),
        -1,
    )
    packed_list = []
    for matrix in range(3):
        chosen = jnp.take(
            to_tiles(shards[matrix], tile_size), jnp.maximum(own_ids[matrix], 0), axis=0
        )
        packed_list.append(
            jnp.where((own_ids[matrix] >= 0)[:, None], chosen, jnp.zeros_like(chosen))
        )
    packed = jnp.stack(packed_list, axis=0)
    all_tiles, all_ids = (
        lax.all_gather(packed, "dp", axis=1, tiled=True),
        lax.all_gather(own_ids, "dp", axis=1, tiled=True),
    )
    slot_total = dp_count * capacity
    anchor = jnp.arange(slot_total, dtype=jnp.int32) // capacity
    global_ids = jnp.where(all_ids >= 0, anchor[None, :] * tile_count + all_ids, -1)
    grid_count = dp_count * tile_count
    grid_index = jnp.arange(grid_count, dtype=jnp.int32)
    holder = global_ids[:, None, :] == grid_index[None, :, None]
    slot_index = jnp.arange(slot_total, dtype=jnp.int32)
    has_tile = jnp.any(holder, axis=2)
    holder_slot = jnp.sum(jnp.where(holder, slot_index[None, None, :], 0), axis=2)
    dense_list = []
    for matrix in range(3):
        chosen = jnp.take(all_tiles[matrix], holder_slot[matrix], axis=0)
        chosen = jnp.where(has_tile[matrix][:, None], chosen, jnp.zeros_like(chosen))
        dense_list.append(from_tiles(chosen, dp_count * row_tiles, col_tiles, tile_size))
    gate_full, up_full, down_full = dense_list
    gate_pre = jnp.dot(full_tokens, gate_full, preferred_element_type=jnp.float32)
    up_pre = jnp.dot(full_tokens, up_full, preferred_element_type=jnp.float32)
    sigmoid_gate = 1.0 / (1.0 + jnp.exp(-gate_pre))
    activated = gate_pre * sigmoid_gate
    hidden = (activated * up_pre).astype(jnp.bfloat16)
    contract_last = (((1,), (1,)), ((), ()))
    output_term = lax.dot_general(
        hidden, down_full, contract_last, preferred_element_type=jnp.float32
    )
    layer_out = lax.psum_scatter(
        output_term.astype(jnp.bfloat16), "mp", scatter_dimension=1, tiled=True
    )
    hidden_grad = jnp.dot(full_cotangent, down_full, preferred_element_type=jnp.float32)
    gate_delta = (
        hidden_grad * up_pre * sigmoid_gate * (1.0 + gate_pre * (1.0 - sigmoid_gate))
    ).astype(jnp.bfloat16)
    up_delta = (hidden_grad * activated).astype(jnp.bfloat16)
    input_term = lax.dot_general(
        gate_delta, gate_full, contract_last, preferred_element_type=jnp.float32
    ) + lax.dot_general(up_delta, up_full, contract_last, preferred_element_type=jnp.float32)
    token_grad = lax.psum_scatter(
        input_term.astype(jnp.bfloat16), "mp", scatter_dimension=1, tiled=True
    )
    left_terms = [full_tokens, full_tokens, full_cotangent]
    right_terms = [gate_delta, up_delta, hidden]
    live_slot = global_ids >= 0
    clipped = jnp.where(live_slot, global_ids, 0)
    blocks_out = []
    for matrix in range(3):
        left_view = left_terms[matrix].reshape(local_rows, dp_count * row_tiles, tile_size)
        right_view = right_terms[matrix].reshape(local_rows, col_tiles, tile_size)
        dense_tiles = jnp.einsum(
            "ria,rjb->ijab", left_view, right_view, preferred_element_type=jnp.float32
        )
        dense_tiles = dense_tiles.reshape(grid_count, tile_size * tile_size)
        chosen = jnp.take(dense_tiles, clipped[matrix], axis=0)
        blocks_out.append(jnp.where(live_slot[matrix][:, None], chosen, 0.0))
    picked = jnp.stack(blocks_out, axis=0)
    summed = lax.psum_scatter(
        picked.reshape(3, dp_count, capacity, tile_size * tile_size).astype(jnp.bfloat16),
        "dp",
        scatter_dimension=1,
        tiled=True,
    ).astype(jnp.float32)
    grad_scale = 1.0 / math.sqrt(local_rows * dp_count)
    own_grads = (summed[:, 0] * grad_scale).astype(jnp.bfloat16)
    grad_shards = []
    for matrix in range(3):
        chosen = jnp.take(own_grads[matrix], own_slot[matrix], axis=0)
        chosen = jnp.where((mask_table[matrix] > 0)[:, None], chosen, jnp.zeros_like(chosen))
        grad_shards.append(from_tiles(chosen, row_tiles, col_tiles, tile_size))
    return (layer_out, token_grad, grad_shards[0], grad_shards[1], grad_shards[2].T)


def solution(mesh):
    placed = (
        P("dp", "mp"),
        P("dp", "mp"),
        P("dp", "mp"),
        P("dp", "mp"),
        P("mp", "dp"),
        P("dp", "mp"),
        P("dp", "mp"),
        P("mp", "dp"),
    )
    return jax.shard_map(
        body,
        mesh=mesh,
        in_specs=placed,
        out_specs=(P("dp", "mp"), P("dp", "mp"), P("dp", "mp"), P("dp", "mp"), P("mp", "dp")),
        check_vma=False,
    )
```

profile of v0, /device:TPU:8, one launch (start us, length us, event | category | flops | bytes accessed | tf_op | source)
XLA Modules:
  0.0 847.9 jit_solution(3259733403799079523)
XLA Ops:
  7.2 0.8 stack_reshape.9
  8.0 0.8 stack_reshape.10
  8.8 0.8 copy.73
  10.3 1.2 reshape.227
  11.9 1.2 reshape.229
  14.4 0.7 gather_fusion
  15.1 0.7 gather_fusion.1
  15.9 0.7 gather_fusion.2
  16.8 1.0 pad_maximum_fusion.1
  17.9 0.7 copy.79
  18.7 0.7 copy.82
  19.5 27.7 %all-gather = s32[8,8,3]{1,2,0:T(4,128)S(1)} all-gather(s32[1,8,3]{1,2,0:T(4,128)S(1)} %bitcast.306), channel_id=1, replica_groups=mesh['dp'=8,'mp'=32] {'dp'}, dimensions={0}, use_global_device_ids=true | all-gather | bytes 864 | tf_op jit(solution)/shard_map/all_gather | solution.py:65
  47.6 103.8 %all-gather.5.cloned.1.call-done = bf16[3,64,16384]{2,1,0:T(8,128)(2,1)} async-done(((bf16[3,8,16384]{2,1,0:T(8,128)(2,1)}), bf16[3,64,16384]{2,1,0:T(8,128)(2,1)}) %all-gather.5.cloned.1.call-update) | async-done | bytes 6291472 | tf_op jit(solution)/shard_map/all_gather | solution.py:64
  151.5 5.4 slice_bitcast_fusion
  156.9 10.6 %gather_fusion.5 = bf16[128,16384]{1,0:T(8,128)(2,1)} fusion(bf16[64,16384]{1,0:T(8,128)(2,1)} %get-tuple-element.37, s32[1024]{0:T(1024)S(1)} %get-tuple-element.74), kind=kCustom, calls=%fused_computation.7.clone | custom fusion | bytes 8389120 | tf_op jit(solution)/shard_map/jit(_take)/gather | solution.py:78
  167.6 2.7 fusion.14
  170.3 3.2 copy.119
  173.5 8.2 copy.81
  181.7 10.6 %gather_fusion.4 = bf16[128,16384]{1,0:T(8,128)(2,1)} fusion(bf16[64,16384]{1,0:T(8,128)(2,1)} %get-tuple-element.38, s32[1024]{0:T(1024)S(1)} %get-tuple-element.75), kind=kCustom, calls=%fused_computation.6.clone | custom fusion | bytes 8389120 | tf_op jit(solution)/shard_map/jit(_take)/gather | solution.py:78
  192.3 2.7 fusion.15
  195.0 3.2 copy.117
  198.2 8.3 copy.80
  206.6 5.2 gather_fusion.3
  211.7 2.7 fusion.16
  214.5 3.2 copy.115
  217.7 8.0 copy.78
  225.7 10.3 %all-gather.7.cloned.1.call-done = bf16[256,4096]{0,1:T(8,128)(2,1)} async-done(((bf16[256,128]{0,1:T(8,128)(2,1)}), bf16[256,4096]{0,1:T(8,128)(2,1)}) %all-gather.7.cloned.1.call-update) | async-done | bytes 2097168 | tf_op jit(solution)/shard_map/all_gather | solution.py:28
  236.0 4.4 fusion.29
  240.8 2.1 fusion.26
  242.9 73.0 %all-gather.9.cloned.1.call-done = bf16[256,4096]{0,1:T(8,128)(2,1)} async-done(((bf16[256,128]{0,1:T(8,128)(2,1)}), bf16[256,4096]{0,1:T(8,128)(2,1)}) %all-gather.9.cloned.1.call-update) | async-done | bytes 2097168 | tf_op jit(solution)/shard_map/all_gather | solution.py:29
  316.0 4.6 multiply_convert_fusion.1
  320.6 3.1 convolution_convert_fusion
  323.7 4.1 copy.106
  327.9 4.1 fusion.7
  332.0 3.3 fusion
  335.3 4.3 copy.108
  339.6 4.9 convolution_bitcast_fusion
  344.5 6.5 copy.90
  351.0 7.7 copy.171
  358.7 3.3 convolution_bitcast_fusion.2
  362.0 6.5 copy.86
  368.5 7.7 copy.173
  376.2 3.3 convolution_bitcast_fusion.1
  379.5 6.7 copy.88
  386.2 7.7 copy.172
  394.0 7.8 gather_fusion.8
  401.8 7.8 gather_fusion.6
  409.5 6.4 gather_fusion.7
  416.0 2.6 fusion.25
  419.6 3.3 pad_maximum_fusion
  423.0 0.6 copy-done.8
  424.4 0.6 dynamic-slice
  425.0 18.8 %reduce-scatter.8.cloned.1.call-done = bf16[128,256]{1,0:T(8,128)(2,1)} async-done(((bf16[4096,256]{1,0:T(8,128)(2,1)}), bf16[128,256]{1,0:T(8,128)(2,1)}) %reduce-scatter.8.cloned.1.call-update) | async-done | bytes 65552
  443.8 1.6 copy.107
  445.4 120.2 %reduce-scatter.10.cloned.1.call-done = bf16[128,256]{1,0:T(8,128)(2,1)} async-done(((bf16[4096,256]{1,0:T(8,128)(2,1)}), bf16[128,256]{1,0:T(8,128)(2,1)}) %reduce-scatter.10.cloned.1.call-update) | async-done | bytes 65552
  565.6 1.6 copy.109
  567.1 264.4 %all-reduce.3.cloned.1.call-done = bf16[3,8,8,16384]{3,2,1,0:T(8,128)(2,1)} async-done(((bf16[3,8,8,16384]{3,2,1,0:T(8,128)(2,1)}), bf16[3,8,8,16384]{3,2,1,0:T(8,128)(2,1)}) %all-reduce.3.cloned.1.call-update) | async-done | bytes 6291472
  831.6 1.9 multiply_convert_fusion
  833.5 0.9 gather_fusion.11
  835.0 0.9 copy.174
  835.9 0.9 gather_fusion.10
  837.4 0.9 copy.175
  838.3 0.9 gather_fusion.9
  839.8 0.9 copy.176
  (97 shorter events, 7.5 us)
Async XLA Ops:
  7.2 6.4 copy-start.5
  7.2 144.3 %all-gather.5.cloned.1.call-start = ((), (), s32[]{:S(2)}) async-start(), calls=%async_computation.2 | async-start | bytes 7077888 | tf_op jit(solution)/shard_map/all_gather | solution.py:64
  15.1 2.8 copy-start.6
  15.1 3.6 copy-start.7
  17.8 218.2 %all-gather.7.cloned.1.call-start = ((), (), s32[]{:S(2)}) async-start(), calls=%async_computation.3 | async-start | bytes 2162688 | tf_op jit(solution)/shard_map/all_gather | solution.py:28
  18.7 297.3 %all-gather.9.cloned.1.call-start = ((), (), s32[]{:S(2)}) async-start(), calls=%async_computation.4 | async-start | bytes 2162688 | tf_op jit(solution)/shard_map/all_gather | solution.py:29
  19.5 424.3 %reduce-scatter.8.cloned.1.call-start = ((), (), s32[]{:S(2)}) async-start(), calls=%async_computation.5 | async-start | bytes 2162688
  236.0 4.4 copy-start
  236.0 4.7 copy-start.3
  316.0 4.6 copy-start.1
  327.8 237.8 %reduce-scatter.10.cloned.1.call-start = ((), (), s32[]{:S(2)}) async-start(), calls=%async_computation.6 | async-start | bytes 2162688
  327.9 4.1 copy-start.2
  393.9 437.6 %all-reduce.3.cloned.1.call-start = ((), (), s32[]{:S(2)}) async-start(), calls=%async_computation.7 | async-start | bytes 12582912
  415.9 2.6 copy-start.4
  422.9 0.7 copy-start.8
  422.9 0.8 copy-start.9
  422.9 0.9 copy-start.10
  422.9 1.5 copy-start.11
Sparse Core Ops, SparseCore 0:
  18.0 133.4 all-gather.4
  154.8 81.1 all-gather.6
  239.4 76.5 all-gather.8
  327.9 115.8 reduce-scatter.7
  448.4 117.1 reduce-scatter.9
  568.1 263.4 all-reduce.2
where the time goes:
time: 858 us; the launch traced here: 848 us
  waiting for transfers between devices  591 us (69%)
  local copies, waits for them, and re-layouts  162 us (19%)
  matrix products  33 us (4%)
  blocking collectives  27.7 us (3%)
  other arithmetic  19.5 us (2%)
  between operations  15.1 us (2%)
    unnamed x9, waiting for transfers between devices  403 us
    all_gather x1, waiting for transfers between devices, body(): lax.all_gather(packed, 'dp', axis=1, tiled=True)  104 us
    all_gather x1, waiting for transfers between devices, body(): lax.all_gather(cotangent, 'mp', axis=1, tiled=True)  73 us
    unnamed x49, local copies, waits for them, and re-layouts  51.6 us
    all_gather x1, blocking collectives, body(): lax.all_gather(own_ids, 'dp', axis=1, tiled=True)  27.7 us
    gather x3, local copies, waits for them, and re-layouts, body(): chosen = jnp.take(all_tiles[matrix], holder_slot[matrix], axis=0)  26.4 us
    reshape x3, local copies, waits for them, and re-layouts, from_tiles(): tile_rows.reshape(row_count, col_count, tile_size, tile_size)  24.5 us
    gather x3, local copies, waits for them, and re-layouts, body(): chosen = jnp.take(dense_tiles, clipped[matrix], axis=0)  21.9 us
  transfers between devices with their start and end apart: 6, of which 6 were waited for; matrix products, arithmetic and copies ran while one was open for 21% of the time, Pallas kernels for 0%

commit v1 on v0

v1 whole, which is shorter than its diff:
```python
import math

import jax
import jax.numpy as jnp
from jax import lax
from jax.experimental import pallas as pl
from jax.experimental.pallas import tpu as pltpu
from jax.sharding import PartitionSpec as P

BLK = 128
F32 = jnp.float32
BF16 = jnp.bfloat16
NX, NZ = 4, 8
SLOTS = 8
TILES = 16
SCALE = 1.0 / math.sqrt(2048)


def kernel(
    tok, cot, gate_w, up_w, down_w, gate_m, up_m, down_m,
    layer_out, token_grad, gate_g, up_g, down_g,
    feats, packed_0, packed_1, packed_2, meta, meta_sm, w_up, w_down, pre, act, psend, precv, hid, deltas,
    tiles, gpack, gtransit, gfinal, gown, outs, ocore, oring, oyh, oyl,
    yl_s, yl_r, yh_s, yh_r, z_s, z_r, c_s, c_r,
    ws_s, wf_s, w_r, meta_s, meta_r, meta_l, p_s, p_r,
    gt_s, gt_r, gf_s, gf_r, oc_s, oc_r, oz_s, oz_r, oyh_s, oyh_r, oyl_s, oyl_r,
):
    dp, mp = lax.axis_index("dp"), lax.axis_index("mp")
    x, yl = dp // 2, dp % 2
    yh, z, c = mp // 16, (mp % 16) // 2, mp % 2

    def dev(dx=0, dz=0, flip_yl=False, flip_yh=False, flip_c=False):
        yl_, yh_, c_ = (1 - yl if flip_yl else yl), (1 - yh if flip_yh else yh), (1 - c if flip_c else c)
        return (((x + dx) % NX) * 2 + yl_, yh_ * 16 + ((z + dz) % NZ) * 2 + c_)

    other_yl, other_yh, other_c = dev(flip_yl=True), dev(flip_yh=True), dev(flip_c=True)
    x_right, x_left, x_far = dev(dx=1), dev(dx=NX - 1), dev(dx=2)
    z_next = (dev(dz=1), dev(dz=NZ - 1))

    def remote(src, dst, send, recv, to):
        return pltpu.make_async_remote_copy(
            src_ref=src, dst_ref=dst, send_sem=send, recv_sem=recv,
            device_id=to, device_id_type=pl.DeviceIdType.MESH,
        )

    def arrived(dst, send, recv):
        remote(dst, dst, send, recv, other_c).wait_recv()

    def loop(n, body):
        def step(i, carry):
            body(i)
            return carry

        lax.fori_loop(0, n, step, 0)

    barrier = pltpu.get_barrier_semaphore()
    partners = (other_yl, other_yh, other_c, x_right, x_left, x_far, *z_next)
    for to in partners:
        pl.semaphore_signal(barrier, inc=1, device_id=to, device_id_type=pl.DeviceIdType.MESH)
    pl.semaphore_wait(barrier, len(partners))

    holder = (z // 2) % 2 == yl

    def holds(at):
        return (at // 2) % 2 == yl

    def chunk(at_yh, at_z, at_c):
        return at_yh * 8 + (at_z // 4) * 4 + (at_z % 2) * 2 + at_c

    home = chunk(yh, z, c)

    def send_z(tc, at_z, w, e, hop):
        q, h = chunk((yh + w) % 2, at_z, c), (yl + e) % 2
        for d in range(2):
            remote(feats.at[tc, q, h], feats.at[tc, q, h], z_s.at[d, hop - 1, tc, w, e], z_r.at[d, hop - 1, tc, w, e], z_next[d]).start()

    def send_core(tc, at_z, w, e):
        q, h = chunk((yh + w) % 2, at_z, c), (yl + e) % 2
        remote(feats.at[tc, q, h], feats.at[tc, q, h], c_s.at[tc, q // 2, e], c_r.at[tc, q // 2, e], other_c).start()

    def yh_piece(tc, e):
        q, h = home, (yl + e) % 2
        return remote(feats.at[tc, q, h], feats.at[tc, q, h], yh_s.at[tc, e], yh_r.at[tc, e], other_yh)

    def tokens_own(tc, ref):
        @pl.when(holder)
        def _():
            feats[tc, home, yl] = ref[...]
            yh_piece(tc, 0).start()
            send_z(tc, z, 0, 0, 1)
            send_core(tc, z, 0, 0)

        @pl.when(jnp.logical_not(holder))
        def _():
            remote(ref, feats.at[tc, home, yl], yl_s.at[tc], yl_r.at[tc], other_yl).start()

    def tokens_second(tc):
        @pl.when(holder)
        def _():
            arrived(feats.at[tc, home, 1 - yl], yl_s.at[tc], yl_r.at[tc])
            yh_piece(tc, 1).start()
            send_z(tc, z, 0, 1, 1)
            send_core(tc, z, 0, 1)

    def tokens_third(tc):
        @pl.when(holder)
        def _():
            for e in range(2):
                arrived(feats.at[tc, chunk(1 - yh, z, c), (yl + e) % 2], yh_s.at[tc, e], yh_r.at[tc, e])
                send_z(tc, z, 1, e, 1)
                send_core(tc, z, 1, e)

    def last_hop(d, w):
        return jnp.where(w == d, 4, 3)

    def tokens_hop(tc, hop):
        def step(i):
            w, e = i // 2, i % 2
            for d in range(2):
                at_z = (z + (NZ - hop if d == 0 else hop)) % NZ

                @pl.when(jnp.logical_and(holds(at_z), hop <= last_hop(d, w)))
                def _():
                    q, h = chunk((yh + w) % 2, at_z, c), (yl + e) % 2
                    piece = feats.at[tc, q, h]
                    arrived(piece, z_s.at[d, hop - 1, tc, w, e], z_r.at[d, hop - 1, tc, w, e])

                    @pl.when(hop < last_hop(d, w))
                    def _():
                        remote(piece, piece, z_s.at[d, hop, tc, w, e], z_r.at[d, hop, tc, w, e], z_next[d]).start()

                    send_core(tc, at_z, w, e)

        loop(4, step)

    def tokens_from_core(tc):
        def step(i):
            j, e = i // 2, i % 2
            arrived(feats.at[tc, j * 2 + 1 - c, (yl + e) % 2], c_s.at[tc, j, e], c_r.at[tc, j, e])

        loop(16, step)

    packed = (packed_0, packed_1, packed_2)
    masks, weights = (gate_m, up_m, down_m), (gate_w, up_w, down_w)
    lane = lax.broadcasted_iota(jnp.int32, (8, BLK), 0) * BLK + lax.broadcasted_iota(jnp.int32, (8, BLK), 1)

    def pack(m, table):
        for t in range(TILES):
            r, k = t // 4, t % 4
            tiles[t] = weights[m][r * BLK:(r + 1) * BLK, k * BLK:(k + 1) * BLK]
        count = jnp.int32(0)
        ids = [jnp.int32(0)] * SLOTS
        for t in range(TILES):
            kept = masks[m][t // 4, t % 4] > 0
            for s in range(min(t + 1, SLOTS)):
                ids[s] = jnp.where(jnp.logical_and(kept, count == s), t, ids[s])
            table = jnp.where(lane == m * BLK + t, jnp.where(kept, count, SLOTS), table)
            count = count + jnp.where(kept, 1, 0)
        for s in range(SLOTS):
            table = jnp.where(lane == m * BLK + TILES + s, ids[s], table)
            packed[m][x, s] = tiles[ids[s]]
        for at, to in ((0, x_right), (1, x_left)):
            for h in range(2):
                half = packed[m].at[x, pl.ds(h * 4, 4)]
                remote(half, half, ws_s.at[at, m, h], w_r.at[at, m, h], to).start()
        return table

    def forward_weights(m):
        for at, h, origin, to in ((0, 0, NX - 1, x_right), (1, 1, 1, x_left)):
            half = packed[m].at[(x + origin) % NX, pl.ds(h * 4, 4)]
            arrived(half, ws_s.at[at, m, h], w_r.at[at, m, h])
            remote(half, half, wf_s.at[m, h], w_r.at[2, m, h], to).start()

    def unpack(m):
        for at, origin in ((0, NX - 1), (1, 1), (2, 2)):
            for h in range(2):
                if at == 2 or at != h:
                    arrived(packed[m].at[(x + origin) % NX, pl.ds(h * 4, 4)], ws_s.at[0, m, h], w_r.at[at, m, h])

        def tile(i):
            xx, r = i // 4, i % 4
            for t in range(4):
                value = packed[m][xx, meta_sm[xx, m, r * 4 + t]]
                if m < 2:
                    row = pl.multiple_of(xx * 512 + r * BLK, BLK)
                    w_up[m, pl.ds(row, BLK), t * BLK:(t + 1) * BLK] = value
                else:
                    w_down[xx, pl.ds(pl.multiple_of(r * BLK, BLK), BLK), t * BLK:(t + 1) * BLK] = value

        loop(16, tile)

    tokens_own(0, tok)
    for xx in range(NX):
        for m in range(3):
            packed[m][xx, SLOTS] = jnp.zeros((BLK, BLK), BF16)
    table = pack(0, jnp.zeros((8, BLK), jnp.int32))
    tokens_own(1, cot)
    tokens_second(0)
    table = pack(1, table)
    table = pack(2, table)
    meta[x] = table
    for at, to in ((0, x_right), (1, x_left), (2, x_far)):
        remote(meta.at[x], meta.at[x], meta_s.at[at], meta_r.at[at], to).start()
    tokens_third(0)
    tokens_hop(0, 1)
    tokens_second(1)
    tokens_hop(0, 2)
    forward_weights(0)
    tokens_third(1)
    tokens_hop(0, 3)
    forward_weights(1)
    for at, origin in ((0, NX - 1), (1, 1), (2, 2)):
        arrived(meta.at[(x + origin) % NX], meta_s.at[at], meta_r.at[at])
    tables = pltpu.make_async_copy(meta, meta_sm, meta_l)
    tables.start()
    tokens_hop(0, 4)
    tables.wait()
    tokens_hop(1, 1)

    def features(tc, h):
        return jnp.concatenate([feats[tc, q, h] for q in range(16)], axis=1)

    def exchange(m):
        def rows(h):
            if m < 2:
                total = jnp.dot(features(0, h), w_up[m], preferred_element_type=F32)
            else:
                total = jnp.zeros((256, 512), F32)
                for xx in range(NX):
                    left = jnp.concatenate([feats[1, xx * 4 + k, h] for k in range(4)], axis=1)
                    total += lax.dot_general(left, w_down[xx], (((1,), (1,)), ((), ())), preferred_element_type=F32)
            pre[m, h] = total
            psend[m, h] = total.astype(BF16)
            remote(psend.at[m, h], precv.at[m, h], p_s.at[m, h], p_r.at[m, h], other_yl).start()

        loop(2, rows)

    def exchanged(m):
        for h in range(2):
            arrived(precv.at[m, h], p_s.at[m, h], p_r.at[m, h])

    tokens_from_core(0)
    unpack(0)
    exchange(0)
    forward_weights(2)
    tokens_hop(1, 2)
    unpack(1)
    exchange(1)
    tokens_hop(1, 3)
    tokens_hop(1, 4)
    tokens_from_core(1)
    unpack(2)
    exchange(2)

    exchanged(0)
    exchanged(1)

    def activate(i):
        h, rows = i // 4, pl.ds(pl.multiple_of((i % 4) * 64, 64), 64)
        g = pre[0, h, rows, :] + precv[0, h, rows, :].astype(F32)
        u = pre[1, h, rows, :] + precv[1, h, rows, :].astype(F32)
        sigmoid = 1.0 / (1.0 + jnp.exp(-g))
        activated = g * sigmoid
        hid[h, rows, :] = (activated * u).astype(BF16)
        act[0, h, rows, :] = u * sigmoid * (1.0 + g * (1.0 - sigmoid))
        act[1, h, rows, :] = activated

    loop(8, activate)

    contract_rows = (((0,), (0,)), ((), ()))

    def grad_partial(m, rel):
        xx = (x + rel) % NX
        side = jnp.concatenate([feats[0 if m < 2 else 1, xx * 4 + k].reshape(512, BLK) for k in range(4)], axis=1)

        def col(k):
            if m < 2:
                right = deltas[m].reshape(512, 512)
                grad = lax.dot_general(side, right, contract_rows, preferred_element_type=F32)
            else:
                grad = lax.dot_general(hid[...].reshape(512, 512), side, contract_rows, preferred_element_type=F32)
            return grad

        grad = col(0).astype(BF16)
        for r in range(4):
            for t in range(4):
                tiles[r * 4 + t] = grad[r * BLK:(r + 1) * BLK, t * BLK:(t + 1) * BLK]
        for s in range(SLOTS):
            gpack[rel, m, s] = tiles[meta_sm[xx, m, TILES + s]]

    lows, highs = pl.ds(0, 4), pl.ds(4, 4)

    def grad_send(m):
        def part(i):
            rel = (i + 2) % NX
            grad_partial(m, rel)

            @pl.when(rel == 2)
            def _():
                remote(gpack.at[2, m, lows], gtransit.at[0, m], gt_s.at[0, m], gt_r.at[0, m], x_right).start()
                remote(gpack.at[2, m, highs], gtransit.at[1, m], gt_s.at[1, m], gt_r.at[1, m], x_left).start()

            @pl.when(rel == 1)
            def _():
                remote(gpack.at[1, m, highs], gfinal.at[0, m, highs], gf_s.at[0, m, 1], gf_r.at[0, m, 1], x_right).start()

            @pl.when(rel == 3)
            def _():
                remote(gpack.at[3, m, lows], gfinal.at[1, m, lows], gf_s.at[1, m, 0], gf_r.at[1, m, 0], x_left).start()

        loop(NX, part)

    def grad_transit(m):
        for at, rel, h, to in ((0, 1, 0, x_right), (1, 3, 1, x_left)):
            part = pl.ds(h * 4, 4)
            arrived(gtransit.at[at, m], gt_s.at[at, m], gt_r.at[at, m])
            gpack[rel, m, part] = (gpack[rel, m, part].astype(F32) + gtransit[at, m].astype(F32)).astype(BF16)
            remote(gpack.at[rel, m, part], gfinal.at[at, m, part], gf_s.at[at, m, h], gf_r.at[at, m, h], to).start()

    def grad_finish(m, out):
        for at in range(2):
            for h in range(2):
                arrived(gfinal.at[at, m, pl.ds(h * 4, 4)], gf_s.at[at, m, h], gf_r.at[at, m, h])
        for s in range(SLOTS):
            total = gpack[0, m, s].astype(F32) + gfinal[0, m, s].astype(F32) + gfinal[1, m, s].astype(F32)
            gown[m, s] = (total * SCALE).astype(BF16)
        gown[m, SLOTS] = jnp.zeros((BLK, BLK), BF16)
        for t in range(TILES):
            r, k = t // 4, t % 4
            out[r * BLK:(r + 1) * BLK, k * BLK:(k + 1) * BLK] = gown[m, meta_sm[x, m, t]]

    def out_partial(o):
        def part(i):
            xx, h = i // 2, i % 2
            if o == 0:
                term = jnp.dot(hid[h], w_down[xx], preferred_element_type=F32)
            else:
                rows = pl.ds(pl.multiple_of(xx * 512, 512), 512)
                along = (((1,), (1,)), ((), ()))
                term = lax.dot_general(deltas[0, h], w_up[0, rows, :], along, preferred_element_type=F32)
                term += lax.dot_general(deltas[1, h], w_up[1, rows, :], along, preferred_element_type=F32)
            term = term.astype(BF16)
            for k in range(4):
                outs[o, xx * 4 + k, h] = term[:, k * BLK:(k + 1) * BLK]

        loop(8, part)

        def send(j):
            remote(outs.at[o, j * 2 + 1 - c], ocore.at[o, j], oc_s.at[o, j], oc_r.at[o, j], other_c).start()

        loop(8, send)

    def out_core(o):
        def step(j):
            arrived(ocore.at[o, j], oc_s.at[o, j], oc_r.at[o, j])
            q = j * 2 + c
            outs[o, q] = (outs[o, q].astype(F32) + ocore[o, j].astype(F32)).astype(BF16)

        loop(8, step)

    def out_hop(o, hop):
        def step(i):
            w, h = i // 2, i % 2
            for d in range(2):
                at_z = (z + (hop if d == 0 else NZ - hop)) % NZ

                @pl.when(jnp.logical_and(holds(at_z), hop <= last_hop(d, w)))
                def _():
                    q = chunk((yh + w) % 2, at_z, c)
                    j = q // 2

                    @pl.when(hop < last_hop(d, w))
                    def _():
                        arrived(oring.at[d, o, j, h], oz_s.at[o, j, h], oz_r.at[d, o, j, h])
                        outs[o, q, h] = (outs[o, q, h].astype(F32) + oring[d, o, j, h].astype(F32)).astype(BF16)

                    remote(outs.at[o, q, h], oring.at[d, o, j, h], oz_s.at[o, j, h], oz_r.at[d, o, j, h], z_next[d]).start()

        loop(4, step)

    def out_home(o):
        @pl.when(holder)
        def _():
            for w in (1, 0):
                for h in range(2):
                    q = chunk((yh + w) % 2, z, c)
                    j = q // 2
                    for d in range(2):
                        arrived(oring.at[d, o, j, h], oz_s.at[o, j, h], oz_r.at[d, o, j, h])
                    total = outs[o, q, h].astype(F32) + oring[0, o, j, h].astype(F32) + oring[1, o, j, h].astype(F32)
                    outs[o, q, h] = total.astype(BF16)
                    if w == 1:
                        remote(outs.at[o, q, h], oyh.at[o, h], oyh_s.at[o, h], oyh_r.at[o, h], other_yh).start()

    def out_last(o, out):
        @pl.when(holder)
        def _():
            for e in (1, 0):
                h = (yl + e) % 2
                arrived(oyh.at[o, h], oyh_s.at[o, h], oyh_r.at[o, h])
                total = (outs[o, home, h].astype(F32) + oyh[o, h].astype(F32)).astype(BF16)
                if e == 1:
                    outs[o, home, h] = total
                    remote(outs.at[o, home, h], oyl.at[o], oyl_s.at[o], oyl_r.at[o], other_yl).start()
                else:
                    out[...] = total

    def out_other(o, out):
        @pl.when(jnp.logical_not(holder))
        def _():
            arrived(oyl.at[o], oyl_s.at[o], oyl_r.at[o])
            out[...] = oyl[o]

    grad_send(2)
    out_partial(0)
    grad_transit(2)
    out_core(0)
    out_hop(0, 4)
    out_hop(0, 3)
    exchanged(2)

    def delta(i):
        h, rows = i // 4, pl.ds(pl.multiple_of((i % 4) * 64, 64), 64)
        hg = pre[2, h, rows, :] + precv[2, h, rows, :].astype(F32)
        deltas[0, h, rows, :] = (hg * act[0, h, rows, :]).astype(BF16)
        deltas[1, h, rows, :] = (hg * act[1, h, rows, :]).astype(BF16)

    loop(8, delta)
    grad_send(0)
    out_hop(0, 2)
    grad_send(1)
    out_hop(0, 1)
    grad_transit(0)
    out_partial(1)
    grad_transit(1)
    out_core(1)
    out_hop(1, 4)
    out_home(0)
    out_hop(1, 3)
    grad_finish(2, down_g)
    out_hop(1, 2)
    out_last(0, layer_out)
    out_hop(1, 1)
    out_home(1)
    grad_finish(0, gate_g)
    grad_finish(1, up_g)
    out_last(1, token_grad)
    out_other(0, layer_out)
    out_other(1, token_grad)

    def left(src, send):
        remote(src, src, send, z_r.at[0, 0, 0, 0, 0], other_c).wait_send()

    piece = feats.at[0, 0, 0]
    for tc in range(2):

        @pl.when(holder)
        def _():
            for e in range(2):
                left(piece, yh_s.at[tc, e])

                for w in range(2):
                    for d in range(2):
                        left(piece, z_s.at[d, 0, tc, w, e])

        @pl.when(jnp.logical_not(holder))
        def _():
            left(piece, yl_s.at[tc])

        def hops(i):
            w, e = i // 2, i % 2
            for hop in range(1, 4):
                for d in range(2):
                    at_z = (z + (NZ - hop if d == 0 else hop)) % NZ

                    @pl.when(jnp.logical_and(holds(at_z), hop < last_hop(d, w)))
                    def _():
                        left(piece, z_s.at[d, hop, tc, w, e])

        loop(4, hops)

        def cores(i):
            left(piece, c_s.at[tc, i // 2, i % 2])

        loop(16, cores)
        o = tc

        def ocores(j):
            left(ocore.at[0, 0], oc_s.at[o, j])

            @pl.when(jnp.logical_not(jnp.logical_and(holder, jnp.logical_and((j // 2) % 2 == z // 4, j % 2 == z % 2))))
            def _():
                for h in range(2):
                    left(piece, oz_s.at[o, j, h])

        loop(8, ocores)

        @pl.when(holder)
        def _():
            for h in range(2):
                left(piece, oyh_s.at[o, h])
            left(piece, oyl_s.at[o])

    half = gtransit.at[0, 0]
    for at in range(3):
        left(meta.at[0], meta_s.at[at])
    for m in range(3):
        for h in range(2):
            for at in range(2):
                left(half, ws_s.at[at, m, h])
                left(half, gf_s.at[at, m, h])
            left(half, wf_s.at[m, h])
            left(half, gt_s.at[h, m])
            left(psend.at[0, 0], p_s.at[m, h])


def body(tokens, cotangent, gate_weight, up_weight, down_weight, gate_mask, up_mask, down_mask):
    vmem, smem = pl.BlockSpec(memory_space=pltpu.VMEM), pl.BlockSpec(memory_space=pltpu.SMEM)
    dma = pltpu.SemaphoreType.DMA
    shapes = (tokens, cotangent, gate_weight, up_weight, down_weight)
    return pl.pallas_call(
        kernel,
        out_shape=tuple(jax.ShapeDtypeStruct(a.shape, a.dtype) for a in shapes),
        in_specs=[vmem] * 5 + [smem] * 3,
        out_specs=(vmem,) * 5,
        scratch_shapes=[
            pltpu.VMEM((2, 16, 2, 256, BLK), BF16),
            *[pltpu.VMEM((NX, SLOTS + 1, BLK, BLK), BF16)] * 3,
            pltpu.VMEM((NX, 8, BLK), jnp.int32),
            pltpu.SMEM((NX, 8, BLK), jnp.int32),
            pltpu.VMEM((2, 2048, 512), BF16),
            pltpu.VMEM((NX, 512, 512), BF16),
            pltpu.VMEM((3, 2, 256, 512), F32),
            pltpu.VMEM((2, 2, 256, 512), F32),
            pltpu.VMEM((3, 2, 256, 512), BF16),
            pltpu.VMEM((3, 2, 256, 512), BF16),
            pltpu.VMEM((2, 256, 512), BF16),
            pltpu.VMEM((2, 2, 256, 512), BF16),
            pltpu.VMEM((TILES, BLK, BLK), BF16),
            pltpu.VMEM((NX, 3, SLOTS, BLK, BLK), BF16),
            pltpu.VMEM((2, 3, 4, BLK, BLK), BF16),
            pltpu.VMEM((2, 3, SLOTS, BLK, BLK), BF16),
            pltpu.VMEM((3, SLOTS + 1, BLK, BLK), BF16),
            pltpu.VMEM((2, 16, 2, 256, BLK), BF16),
            pltpu.VMEM((2, 8, 2, 256, BLK), BF16),
            pltpu.VMEM((2, 2, 8, 2, 256, BLK), BF16),
            pltpu.VMEM((2, 2, 256, BLK), BF16),
            pltpu.VMEM((2, 256, BLK), BF16),
            dma((2,)), dma((2,)), dma((2, 2)), dma((2, 2)),
            dma((2, 4, 2, 2, 2)), dma((2, 4, 2, 2, 2)),
            dma((2, 8, 2)), dma((2, 8, 2)),
            dma((2, 3, 2)), dma((3, 2)), dma((3, 3, 2)),
            dma((3,)), dma((3,)), dma(()),
            dma((3, 2)), dma((3, 2)),
            dma((2, 3)), dma((2, 3)), dma((2, 3, 2)), dma((2, 3, 2)),
            dma((2, 8)), dma((2, 8)),
            dma((2, 8, 2)), dma((2, 2, 8, 2)),
            dma((2, 2)), dma((2, 2)), dma((2,)), dma((2,)),
        ],
        compiler_params=pltpu.CompilerParams(
            collective_id=0, has_side_effects=True, vmem_limit_bytes=58 * 2**20
        ),
        cost_estimate=pl.CostEstimate(flops=9_663_676_416, bytes_accessed=4 * 2**20, transcendentals=262144),
    )(tokens, cotangent, gate_weight, up_weight, down_weight, gate_mask, up_mask, down_mask)


def solution(mesh):
    up, down = P("dp", "mp"), P("mp", "dp")
    return jax.shard_map(
        body,
        mesh=mesh,
        in_specs=(up, up, up, up, down, up, up, down),
        out_specs=(up, up, up, up, down),
        check_vma=False,
    )
```

time: 858 us -> 130 us (0.15); the launches traced: 848 us -> 130 us
  waiting for transfers between devices: 591 us -> 0 us
  local copies, waits for them, and re-layouts: 162 us -> 6.09 us
  Pallas kernels: 0 us -> 123 us
  matrix products: 33 us -> 0 us
  blocking collectives: 27.7 us -> 0 us
  other arithmetic: 19.5 us -> 0 us
  between operations: 15.1 us -> 0.65 us
    unnamed x9 -> x0, waiting for transfers between devices: 403 us -> none
    all_gather x3 -> x0, waiting for transfers between devices: 187 us -> none  [the longest x1 104 us: body(): lax.all_gather(packed, 'dp', axis=1, tiled=True)]
    pallas_call x0 -> x1, Pallas kernels: none -> 123 us  [body(): pl.pallas_call(kernel, out_shape=tuple((jax.ShapeDtypeStruct(a.shape, a.d...]
    gather x12 -> x0, local copies, waits for them, and re-layouts: 53.1 us -> none  [the longest x3 26.4 us: body(): chosen = jnp.take(all_tiles[matrix], holder_slot[matrix], axis=0)]
    unnamed x49 -> x11, local copies, waits for them, and re-layouts: 51.6 us -> 6.09 us
    dot_general x9 -> x0, matrix products: 33 us -> none  [the longest x3 11.4 us: body(): jnp.einsum('ria,rjb->ijab', left_view, right_view, preferred_element_type...]
    all_gather x1 -> x0, blocking collectives: 27.7 us -> none  [body(): lax.all_gather(own_ids, 'dp', axis=1, tiled=True)]
    reshape x9 -> x0, local copies, waits for them, and re-layouts: 27.6 us -> none  [the longest x3 24.5 us: from_tiles(): tile_rows.reshape(row_count, col_count, tile_size, tile_size)]
  transfers between devices with their start and end apart: 6 -> 0, of which waited for: 6 -> 0; matrix products, arithmetic and copies ran while one was open for 21% -> 0% of each run, Pallas kernels for 0% -> 0%
where the time goes in v1:
time: 130 us
  Pallas kernels  123 us (95%)
  local copies, waits for them, and re-layouts  6.09 us (5%)
    pallas_call x1, Pallas kernels, body(): pl.pallas_call(kernel, out_shape=tuple((jax.ShapeDtypeStruct(a.shape, a.d...  123 us
    unnamed x11, local copies, waits for them, and re-layouts  6.09 us

profile of v1, /device:TPU:8, one launch (start us, length us, event | category | flops | bytes accessed | tf_op | source)
XLA Modules:
  0.0 129.9 jit_solution(3020265114180945318)
XLA Ops:
  0.6 123.1 %shard_map.119 = (bf16[256,128]{1,0:T(8,128)(2,1)}, bf16[256,128]{1,0:T(8,128)(2,1)}, bf16[512,512]{1,0:T(8,128)(2,1)}, bf16[512,512]{1,0:T(8,128)(2,1)}, bf16[512,512]{1,0:T(8,128)(2,1)}) custom-call(bf16[256,128]{1,0:T(8,128)(2,1)} %tok.1, bf16[256,128]{1,0:T(8,128)(2,1)} %cot.1, bf16[512,512]{1,0:T(8,128)(2,1)} %gate_w.1, bf16[512,512]{1,0:T(8,128)(2,1)} %up_w.1, ...), custom_call_target="tpu_custom_call" | custom-call | flops 9663676416 | bytes 4194304 | tf_op jit(solution)/shard_map/pallas_call | solution.py:521
  123.8 0.0 copy-start.2
  123.8 1.5 %copy.18 = bf16[256,128]{1,0:T(8,128)(2,1)} copy(bf16[256,128]{1,0:T(8,128)(2,1)} %get-tuple-element.10) | data formatting | bytes 131072
  125.3 0.0 copy-done.2
  125.3 0.6 copy.19
  125.9 0.0 copy-start.1
  125.9 1.9 %copy.20 = bf16[512,512]{1,0:T(8,128)(2,1)} copy(bf16[512,512]{1,0:T(8,128)(2,1)} %get-tuple-element.12) | data formatting | bytes 1048576
  127.9 0.0 copy-done.1
  127.9 0.0 copy-start
  127.9 0.8 copy.21
  128.7 0.4 copy-done
  129.1 0.8 copy.22
Async XLA Ops:
  123.8 1.5 %copy-start.2 = (bf16[256,128]{1,0:T(8,128)(2,1)S(1)}, bf16[256,128]{1,0:T(8,128)(2,1)}, u32[]{:S(2)}) copy-start(bf16[256,128]{1,0:T(8,128)(2,1)} %get-tuple-element.11) | copy-start | bytes 196612
  125.9 1.9 %copy-start.1 = (bf16[512,512]{1,0:T(8,128)(2,1)S(1)}, bf16[512,512]{1,0:T(8,128)(2,1)}, u32[]{:S(2)}) copy-start(bf16[512,512]{1,0:T(8,128)(2,1)} %get-tuple-element.13) | copy-start | bytes 1572868
  127.9 1.2 copy-start

commit v2 on v1

--- a/solution.py
+++ b/solution.py
@@ -20,10 +20,10 @@
     tok, cot, gate_w, up_w, down_w, gate_m, up_m, down_m,
     layer_out, token_grad, gate_g, up_g, down_g,
     feats, packed_0, packed_1, packed_2, meta, meta_sm, w_up, w_down, pre, act, psend, precv, hid, deltas,
-    tiles, gpack, gtransit, gfinal, gown, outs, ocore, oring, oyh, oyl,
+    tiles, gpack, gtransit, gfinal, gown, outs, ocore, oring, ohome, oyh, oyl,
     yl_s, yl_r, yh_s, yh_r, z_s, z_r, c_s, c_r,
     ws_s, wf_s, w_r, meta_s, meta_r, meta_l, p_s, p_r,
-    gt_s, gt_r, gf_s, gf_r, oc_s, oc_r, oz_s, oz_r, oyh_s, oyh_r, oyl_s, oyl_r,
+    gt_s, gt_r, gf_s, gf_r, oc_s, oc_r, oz_s, oz_r, oh_s, oh_r, oyh_s, oyh_r, oyl_s, oyl_r,
 ):
     dp, mp = lax.axis_index("dp"), lax.axis_index("mp")
     x, yl = dp // 2, dp % 2
@@ -35,7 +35,8 @@
 
     other_yl, other_yh, other_c = dev(flip_yl=True), dev(flip_yh=True), dev(flip_c=True)
     x_right, x_left, x_far = dev(dx=1), dev(dx=NX - 1), dev(dx=2)
-    z_next = (dev(dz=1), dev(dz=NZ - 1))
+    z_up, z_down = dev(dz=1), dev(dz=NZ - 1)
+    z_to = dev(dz=jnp.where(c == 0, 1, NZ - 1))
 
     def remote(src, dst, send, recv, to):
         return pltpu.make_async_remote_copy(
@@ -54,7 +55,7 @@
         lax.fori_loop(0, n, step, 0)
 
     barrier = pltpu.get_barrier_semaphore()
-    partners = (other_yl, other_yh, other_c, x_right, x_left, x_far, *z_next)
+    partners = (other_yl, other_yh, other_c, x_right, x_left, x_far, z_up, z_down)
     for to in partners:
         pl.semaphore_signal(barrier, inc=1, device_id=to, device_id_type=pl.DeviceIdType.MESH)
     pl.semaphore_wait(barrier, len(partners))
@@ -69,76 +70,101 @@
 
     home = chunk(yh, z, c)
 
-    def send_z(tc, at_z, w, e, hop):
-        q, h = chunk((yh + w) % 2, at_z, c), (yl + e) % 2
-        for d in range(2):
-            remote(feats.at[tc, q, h], feats.at[tc, q, h], z_s.at[d, hop - 1, tc, w, e], z_r.at[d, hop - 1, tc, w, e], z_next[d]).start()
-
-    def send_core(tc, at_z, w, e):
-        q, h = chunk((yh + w) % 2, at_z, c), (yl + e) % 2
-        remote(feats.at[tc, q, h], feats.at[tc, q, h], c_s.at[tc, q // 2, e], c_r.at[tc, q // 2, e], other_c).start()
-
-    def yh_piece(tc, e):
-        q, h = home, (yl + e) % 2
-        return remote(feats.at[tc, q, h], feats.at[tc, q, h], yh_s.at[tc, e], yh_r.at[tc, e], other_yh)
+    def behind(hops):
+        return (z + jnp.where(c == 0, NZ - hops, hops)) % NZ
+
+    def ahead(hops):
+        return (z + jnp.where(c == 0, hops, NZ - hops)) % NZ
+
+    def last_hop(w):
+        return jnp.where(w == c, 4, 3)
+
+    def by_core(up, w):
+        return jnp.where(up <= jnp.where(w == 0, 4, 3), 0, 1)
+
+    def send_core(tc, q, e):
+        piece = feats.at[tc, q, (yl + e) % 2]
+        remote(piece, piece, c_s.at[tc, q, e], c_r.at[tc, q, e], other_c).start()
+
+    def send_yh(tc, e):
+        piece = feats.at[tc, home, (yl + e) % 2]
+        remote(piece, piece, yh_s.at[tc, e], yh_r.at[tc, e], other_yh).start()
 
     def tokens_own(tc, ref):
         @pl.when(holder)
         def _():
             feats[tc, home, yl] = ref[...]
-            yh_piece(tc, 0).start()
-            send_z(tc, z, 0, 0, 1)
-            send_core(tc, z, 0, 0)
+            send_yh(tc, 0)
 
         @pl.when(jnp.logical_not(holder))
         def _():
             remote(ref, feats.at[tc, home, yl], yl_s.at[tc], yl_r.at[tc], other_yl).start()
 
-    def tokens_second(tc):
-        @pl.when(holder)
-        def _():
-            arrived(feats.at[tc, home, 1 - yl], yl_s.at[tc], yl_r.at[tc])
-            yh_piece(tc, 1).start()
-            send_z(tc, z, 0, 1, 1)
-            send_core(tc, z, 0, 1)
-
-    def tokens_third(tc):
-        @pl.when(holder)
-        def _():
-            for e in range(2):
-                arrived(feats.at[tc, chunk(1 - yh, z, c), (yl + e) % 2], yh_s.at[tc, e], yh_r.at[tc, e])
-                send_z(tc, z, 1, e, 1)
-                send_core(tc, z, 1, e)
-
-    def last_hop(d, w):
-        return jnp.where(w == d, 4, 3)
-
-    def tokens_hop(tc, hop):
-        def step(i):
-            w, e = i // 2, i % 2
-            for d in range(2):
-                at_z = (z + (NZ - hop if d == 0 else hop)) % NZ
-
-                @pl.when(jnp.logical_and(holds(at_z), hop <= last_hop(d, w)))
+    def token_waves(first, end):
+        def wave(t, carry):
+            def send_z(piece, tc, w, e, o, hop):
+                remote(piece, piece, z_s.at[hop, tc, w, e, o], z_r.at[hop, tc, w, e, o], z_to).start()
+
+            @pl.when(jnp.logical_and(holder, t < 16))
+            def _():
+                tc, w, e, o = t // 8, (t // 4) % 2, (t // 2) % 2, t % 2
+                q = chunk((yh + w) % 2, z, (c + o) % 2)
+                piece = feats.at[tc, q, (yl + e) % 2]
+
+                @pl.when(o == 1)
                 def _():
-                    q, h = chunk((yh + w) % 2, at_z, c), (yl + e) % 2
-                    piece = feats.at[tc, q, h]
-                    arrived(piece, z_s.at[d, hop - 1, tc, w, e], z_r.at[d, hop - 1, tc, w, e])
-
-                    @pl.when(hop < last_hop(d, w))
+                    arrived(piece, c_s.at[tc, q, e], c_r.at[tc, q, e])
+
+                @pl.when(o == 0)
+                def _():
+                    @pl.when(jnp.logical_and(w == 0, e == 1))
                     def _():
-                        remote(piece, piece, z_s.at[d, hop, tc, w, e], z_r.at[d, hop, tc, w, e], z_next[d]).start()
-
-                    send_core(tc, at_z, w, e)
-
-        loop(4, step)
+                        arrived(piece, yl_s.at[tc], yl_r.at[tc])
+                        send_yh(tc, 1)
+
+                    @pl.when(w == 1)
+                    def _():
+                        arrived(piece, yh_s.at[tc, e], yh_r.at[tc, e])
+
+                    send_core(tc, q, e)
+
+                send_z(piece, tc, w, e, o, 0)
+
+            for hop in (4, 3, 2, 1):
+                p, at_z = t - 2 * hop, behind(hop)
+                tc, w, e, o = p // 8, (p // 4) % 2, (p // 2) % 2, p % 2
+                takes = jnp.logical_and(holds(at_z), hop <= last_hop(w))
+
+                @pl.when(jnp.logical_and(takes, jnp.logical_and(p >= 0, p < 16)))
+                def _():
+                    q = chunk((yh + w) % 2, at_z, (c + o) % 2)
+                    piece = feats.at[tc, q, (yl + e) % 2]
+                    arrived(piece, z_s.at[hop - 1, tc, w, e, o], z_r.at[hop - 1, tc, w, e, o])
+                    if hop < 4:
+
+                        @pl.when(hop < last_hop(w))
+                        def _():
+                            send_z(piece, tc, w, e, o, hop)
+
+                    send_core(tc, q, e)
+
+            return carry
+
+        lax.fori_loop(first, end, wave, 0)
+
+    def via_core(j):
+        up = (z - ((j // 2) % 2 * 4 + yl * 2 + j % 2) + NZ) % NZ
+        return jnp.logical_and(up != 0, by_core(up, (j // 4 + yh) % 2) != c)
 
     def tokens_from_core(tc):
         def step(i):
-            j, e = i // 2, i % 2
-            arrived(feats.at[tc, j * 2 + 1 - c, (yl + e) % 2], c_s.at[tc, j, e], c_r.at[tc, j, e])
-
-        loop(16, step)
+            q, e = i // 2, i % 2
+
+            @pl.when(via_core(q // 2))
+            def _():
+                arrived(feats.at[tc, q, (yl + e) % 2], c_s.at[tc, q, e], c_r.at[tc, q, e])
+
+        loop(32, step)
 
     packed = (packed_0, packed_1, packed_2)
     masks, weights = (gate_m, up_m, down_m), (gate_w, up_w, down_w)
@@ -190,32 +216,33 @@
         loop(16, tile)
 
     tokens_own(0, tok)
-    for xx in range(NX):
-        for m in range(3):
-            packed[m][xx, SLOTS] = jnp.zeros((BLK, BLK), BF16)
+    tokens_own(1, cot)
+    token_waves(0, 1)
     table = pack(0, jnp.zeros((8, BLK), jnp.int32))
-    tokens_own(1, cot)
-    tokens_second(0)
+    token_waves(1, 2)
     table = pack(1, table)
+    token_waves(2, 4)
     table = pack(2, table)
     meta[x] = table
     for at, to in ((0, x_right), (1, x_left), (2, x_far)):
         remote(meta.at[x], meta.at[x], meta_s.at[at], meta_r.at[at], to).start()
-    tokens_third(0)
-    tokens_hop(0, 1)
-    tokens_second(1)
-    tokens_hop(0, 2)
+    token_waves(4, 6)
+    for xx in range(NX):
+        for m in range(3):
+            packed[m][xx, SLOTS] = jnp.zeros((BLK, BLK), BF16)
+    token_waves(6, 8)
     forward_weights(0)
-    tokens_third(1)
-    tokens_hop(0, 3)
-    forward_weights(1)
+    token_waves(8, 10)
     for at, origin in ((0, NX - 1), (1, 1), (2, 2)):
         arrived(meta.at[(x + origin) % NX], meta_s.at[at], meta_r.at[at])
     tables = pltpu.make_async_copy(meta, meta_sm, meta_l)
     tables.start()
-    tokens_hop(0, 4)
+    token_waves(10, 13)
     tables.wait()
-    tokens_hop(1, 1)
+    unpack(0)
+    token_waves(13, 15)
+    forward_weights(1)
+    token_waves(15, 16)
 
     def features(tc, h):
         return jnp.concatenate([feats[tc, q, h] for q in range(16)], axis=1)
@@ -240,14 +267,13 @@
             arrived(precv.at[m, h], p_s.at[m, h], p_r.at[m, h])
 
     tokens_from_core(0)
-    unpack(0)
     exchange(0)
-    forward_weights(2)
-    tokens_hop(1, 2)
+    token_waves(16, 18)
     unpack(1)
     exchange(1)
-    tokens_hop(1, 3)
-    tokens_hop(1, 4)
+    token_waves(18, 20)
+    forward_weights(2)
+    token_waves(20, 24)
     tokens_from_core(1)
     unpack(2)
     exchange(2)
@@ -346,49 +372,66 @@
         loop(8, part)
 
         def send(j):
-            remote(outs.at[o, j * 2 + 1 - c], ocore.at[o, j], oc_s.at[o, j], oc_r.at[o, j], other_c).start()
+            @pl.when(out_via_core(j))
+            def _():
+                pair = pl.ds(j * 2, 2)
+                remote(outs.at[o, pair], ocore.at[o, j], oc_s.at[o, j], oc_r.at[o, j], other_c).start()
 
         loop(8, send)
 
-    def out_core(o):
-        def step(j):
-            arrived(ocore.at[o, j], oc_s.at[o, j], oc_r.at[o, j])
-            q = j * 2 + c
-            outs[o, q] = (outs[o, q].astype(F32) + ocore[o, j].astype(F32)).astype(BF16)
-
-        loop(8, step)
-
-    def out_hop(o, hop):
-        def step(i):
-            w, h = i // 2, i % 2
-            for d in range(2):
-                at_z = (z + (hop if d == 0 else NZ - hop)) % NZ
-
-                @pl.when(jnp.logical_and(holds(at_z), hop <= last_hop(d, w)))
+    def out_via_core(j):
+        up = ((j // 2) % 2 * 4 + yl * 2 + j % 2 - z + NZ) % NZ
+        return jnp.logical_and(up != 0, by_core(up, (j // 4 + yh) % 2) != c)
+
+    def out_waves(o, first, end):
+        def wave(t, carry):
+            for hop in (4, 1, 2, 3):
+                p, at_z = t - 2 * (4 - hop), ahead(hop)
+                w, cc, h = 1 - p // 4, (p // 2) % 2, p % 2
+                takes = jnp.logical_and(holds(at_z), hop <= last_hop(w))
+
+                @pl.when(jnp.logical_and(takes, jnp.logical_and(p >= 0, p < 8)))
                 def _():
-                    q = chunk((yh + w) % 2, at_z, c)
-                    j = q // 2
-
-                    @pl.when(hop < last_hop(d, w))
+                    j = chunk((yh + w) % 2, at_z, 0) // 2
+                    q = j * 2 + cc
+
+                    @pl.when(p % 4 == 0)
                     def _():
-                        arrived(oring.at[d, o, j, h], oz_s.at[o, j, h], oz_r.at[d, o, j, h])
-                        outs[o, q, h] = (outs[o, q, h].astype(F32) + oring[d, o, j, h].astype(F32)).astype(BF16)
-
-                    remote(outs.at[o, q, h], oring.at[d, o, j, h], oz_s.at[o, j, h], oz_r.at[d, o, j, h], z_next[d]).start()
-
-        loop(4, step)
+                        arrived(ocore.at[o, j], oc_s.at[o, j], oc_r.at[o, j])
+
+                    total = outs[o, q, h].astype(F32) + ocore[o, j, cc, h].astype(F32)
+                    outs[o, q, h] = total.astype(BF16)
+                    if hop < 4:
+
+                        @pl.when(hop < last_hop(w))
+                        def _():
+                            arrived(oring.at[o, j, cc, h], oz_s.at[o, j, cc, h], oz_r.at[o, j, cc, h])
+                            outs[o, q, h] = (total + oring[o, j, cc, h].astype(F32)).astype(BF16)
+
+                    remote(outs.at[o, q, h], oring.at[o, j, cc, h], oz_s.at[o, j, cc, h], oz_r.at[o, j, cc, h], z_to).start()
+
+            return carry
+
+        lax.fori_loop(first, end, wave, 0)
 
     def out_home(o):
         @pl.when(holder)
         def _():
             for w in (1, 0):
+                j = chunk((yh + w) % 2, z, 0) // 2
+                for own in (0, 1):
+                    cc = (c + 1 - own) % 2
+                    for h in range(2):
+                        q = j * 2 + cc
+                        arrived(oring.at[o, j, cc, h], oz_s.at[o, j, cc, h], oz_r.at[o, j, cc, h])
+                        outs[o, q, h] = (outs[o, q, h].astype(F32) + oring[o, j, cc, h].astype(F32)).astype(BF16)
+                        if own == 0:
+                            remote(outs.at[o, q, h], ohome.at[o, w, h], oh_s.at[o, w, h], oh_r.at[o, w, h], other_c).start()
+            for w in (1, 0):
+                q = chunk((yh + w) % 2, z, c)
                 for h in range(2):
-                    q = chunk((yh + w) % 2, z, c)
-                    j = q // 2
-                    for d in range(2):
-                        arrived(oring.at[d, o, j, h], oz_s.at[o, j, h], oz_r.at[d, o, j, h])
-                    total = outs[o, q, h].astype(F32) + oring[0, o, j, h].astype(F32) + oring[1, o, j, h].astype(F32)
-                    outs[o, q, h] = total.astype(BF16)
+                    arrived(ohome.at[o, w, h], oh_s.at[o, w, h], oh_r.at[o, w, h])
+                    outs[o, q, h] = (outs[o, q, h].astype(F32) + ohome[o, w, h].astype(F32)).astype(BF16)
                     if w == 1:
                         remote(outs.at[o, q, h], oyh.at[o, h], oyh_s.at[o, h], oyh_r.at[o, h], other_yh).start()
 
@@ -411,12 +454,11 @@
             arrived(oyl.at[o], oyl_s.at[o], oyl_r.at[o])
             out[...] = oyl[o]
 
+    out_partial(0)
     grad_send(2)
-    out_partial(0)
+    out_waves(0, 0, 6)
     grad_transit(2)
-    out_core(0)
-    out_hop(0, 4)
-    out_hop(0, 3)
+    out_waves(0, 6, 14)
     exchanged(2)
 
     def delta(i):
@@ -427,24 +469,21 @@
 
     loop(8, delta)
     grad_send(0)
-    out_hop(0, 2)
+    out_partial(1)
+    out_waves(1, 0, 2)
     grad_send(1)
-    out_hop(0, 1)
+    out_waves(1, 2, 6)
     grad_transit(0)
-    out_partial(1)
+    out_waves(1, 6, 10)
     grad_transit(1)
-    out_core(1)
-    out_hop(1, 4)
+    out_waves(1, 10, 14)
     out_home(0)
-    out_hop(1, 3)
+    out_home(1)
+    out_last(0, layer_out)
+    out_last(1, token_grad)
     grad_finish(2, down_g)
-    out_hop(1, 2)
-    out_last(0, layer_out)
-    out_hop(1, 1)
-    out_home(1)
     grad_finish(0, gate_g)
     grad_finish(1, up_g)
-    out_last(1, token_grad)
     out_other(0, layer_out)
     out_other(1, token_grad)
 
@@ -452,54 +491,58 @@
         remote(src, src, send, z_r.at[0, 0, 0, 0, 0], other_c).wait_send()
 
     piece = feats.at[0, 0, 0]
+
+    def tokens_left(i):
+        tc, w, e, o = i // 8, (i // 4) % 2, (i // 2) % 2, i % 2
+        for hop in range(4):
+            at_z = behind(hop)
+
+            @pl.when(jnp.logical_and(holds(at_z), hop < last_hop(w)))
+            def _():
+                left(piece, z_s.at[hop, tc, w, e, o])
+
+    loop(16, tokens_left)
+
+    def to_core_left(i):
+        tc, q, e = i // 32, (i // 2) % 16, i % 2
+        own = jnp.logical_and((q // 4) % 2 * 4 + yl * 2 + (q // 2) % 2 == z, q % 2 != c)
+
+        @pl.when(jnp.logical_not(jnp.logical_or(via_core(q // 2), own)))
+        def _():
+            left(piece, c_s.at[tc, q, e])
+
+    loop(64, to_core_left)
+
+    def outs_left(i):
+        o, j = i // 8, i % 8
+        at_home = (j // 2) % 2 * 4 + yl * 2 + j % 2 == z
+        other = out_via_core(j)
+
+        @pl.when(other)
+        def _():
+            left(ocore.at[0, 0], oc_s.at[o, j])
+
+        @pl.when(jnp.logical_not(jnp.logical_or(other, at_home)))
+        def _():
+            for cc in range(2):
+                for h in range(2):
+                    left(piece, oz_s.at[o, j, cc, h])
+
+    loop(16, outs_left)
     for tc in range(2):
 
         @pl.when(holder)
         def _():
             for e in range(2):
                 left(piece, yh_s.at[tc, e])
-
+                left(piece, oyh_s.at[tc, e])
                 for w in range(2):
-                    for d in range(2):
-                        left(piece, z_s.at[d, 0, tc, w, e])
+                    left(piece, oh_s.at[tc, w, e])
+            left(piece, oyl_s.at[tc])
 
         @pl.when(jnp.logical_not(holder))
         def _():
             left(piece, yl_s.at[tc])
-
-        def hops(i):
-            w, e = i // 2, i % 2
-            for hop in range(1, 4):
-                for d in range(2):
-                    at_z = (z + (NZ - hop if d == 0 else hop)) % NZ
-
-                    @pl.when(jnp.logical_and(holds(at_z), hop < last_hop(d, w)))
-                    def _():
-                        left(piece, z_s.at[d, hop, tc, w, e])
-
-        loop(4, hops)
-
-        def cores(i):
-            left(piece, c_s.at[tc, i // 2, i % 2])
-
-        loop(16, cores)
-        o = tc
-
-        def ocores(j):
-            left(ocore.at[0, 0], oc_s.at[o, j])
-
-            @pl.when(jnp.logical_not(jnp.logical_and(holder, jnp.logical_and((j // 2) % 2 == z // 4, j % 2 == z % 2))))
-            def _():
-                for h in range(2):
-                    left(piece, oz_s.at[o, j, h])
-
-        loop(8, ocores)
-
-        @pl.when(holder)
-        def _():
-            for h in range(2):
-                left(piece, oyh_s.at[o, h])
-            left(piece, oyl_s.at[o])
 
     half = gtransit.at[0, 0]
     for at in range(3):
@@ -542,19 +585,21 @@
             pltpu.VMEM((2, 3, SLOTS, BLK, BLK), BF16),
             pltpu.VMEM((3, SLOTS + 1, BLK, BLK), BF16),
             pltpu.VMEM((2, 16, 2, 256, BLK), BF16),
-            pltpu.VMEM((2, 8, 2, 256, BLK), BF16),
-            pltpu.VMEM((2, 2, 8, 2, 256, BLK), BF16),
+            pltpu.VMEM((2, 8, 2, 2, 256, BLK), BF16),
+            pltpu.VMEM((2, 8, 2, 2, 256, BLK), BF16),
+            pltpu.VMEM((2, 2, 2, 256, BLK), BF16),
             pltpu.VMEM((2, 2, 256, BLK), BF16),
             pltpu.VMEM((2, 256, BLK), BF16),
             dma((2,)), dma((2,)), dma((2, 2)), dma((2, 2)),
-            dma((2, 4, 2, 2, 2)), dma((2, 4, 2, 2, 2)),
-            dma((2, 8, 2)), dma((2, 8, 2)),
+            dma((4, 2, 2, 2, 2)), dma((4, 2, 2, 2, 2)),
+            dma((2, 16, 2)), dma((2, 16, 2)),
             dma((2, 3, 2)), dma((3, 2)), dma((3, 3, 2)),
             dma((3,)), dma((3,)), dma(()),
             dma((3, 2)), dma((3, 2)),
             dma((2, 3)), dma((2, 3)), dma((2, 3, 2)), dma((2, 3, 2)),
             dma((2, 8)), dma((2, 8)),
-            dma((2, 8, 2)), dma((2, 2, 8, 2)),
+            dma((2, 8, 2, 2)), dma((2, 8, 2, 2)),
+            dma((2, 2, 2)), dma((2, 2, 2)),
             dma((2, 2)), dma((2, 2)), dma((2,)), dma((2,)),
         ],
         compiler_params=pltpu.CompilerParams(

time: 130 us -> 147 us (1.13)
  Pallas kernels: 123 us -> 140 us
    pallas_call x1, Pallas kernels: 123 us -> 140 us  [body(): pl.pallas_call(kernel, out_shape=tuple((jax.ShapeDtypeStruct(a.shape, a.d...]
where the time goes in v2:
time: 147 us
  Pallas kernels  140 us (95%)
  local copies, waits for them, and re-layouts  6.09 us (4%)
    pallas_call x1, Pallas kernels, body(): pl.pallas_call(kernel, out_shape=tuple((jax.ShapeDtypeStruct(a.shape, a.d...  140 us
    unnamed x11, local copies, waits for them, and re-layouts  6.09 us

profile of v2, /device:TPU:8, one launch (start us, length us, event | category | flops | bytes accessed | tf_op | source)
XLA Modules:
  0.0 146.5 jit_solution(17674893789248905931)
XLA Ops:
  0.6 139.8 %shard_map.119 = (bf16[256,128]{1,0:T(8,128)(2,1)}, bf16[256,128]{1,0:T(8,128)(2,1)}, bf16[512,512]{1,0:T(8,128)(2,1)}, bf16[512,512]{1,0:T(8,128)(2,1)}, bf16[512,512]{1,0:T(8,128)(2,1)}) custom-call(bf16[256,128]{1,0:T(8,128)(2,1)} %tok.1, bf16[256,128]{1,0:T(8,128)(2,1)} %cot.1, bf16[512,512]{1,0:T(8,128)(2,1)} %gate_w.1, bf16[512,512]{1,0:T(8,128)(2,1)} %up_w.1, ...), custom_call_target="tpu_custom_call" | custom-call | flops 9663676416 | bytes 4194304 | tf_op jit(solution)/shard_map/pallas_call | solution.py:564
  140.4 0.0 copy-start.2
  140.4 1.5 %copy.18 = bf16[256,128]{1,0:T(8,128)(2,1)} copy(bf16[256,128]{1,0:T(8,128)(2,1)} %get-tuple-element.10) | data formatting | bytes 131072
  141.9 0.0 copy-done.2
  141.9 0.6 copy.19
  142.5 0.0 copy-start.1
  142.5 1.9 %copy.20 = bf16[512,512]{1,0:T(8,128)(2,1)} copy(bf16[512,512]{1,0:T(8,128)(2,1)} %get-tuple-element.12) | data formatting | bytes 1048576
  144.5 0.0 copy-done.1
  144.5 0.0 copy-start
  144.5 0.8 copy.21
  145.3 0.4 copy-done
  145.7 0.8 copy.22
Async XLA Ops:
  140.4 1.5 %copy-start.2 = (bf16[256,128]{1,0:T(8,128)(2,1)S(1)}, bf16[256,128]{1,0:T(8,128)(2,1)}, u32[]{:S(2)}) copy-start(bf16[256,128]{1,0:T(8,128)(2,1)} %get-tuple-element.11) | copy-start | bytes 196612
  142.5 1.9 %copy-start.1 = (bf16[512,512]{1,0:T(8,128)(2,1)S(1)}, bf16[512,512]{1,0:T(8,128)(2,1)}, u32[]{:S(2)}) copy-start(bf16[512,512]{1,0:T(8,128)(2,1)} %get-tuple-element.13) | copy-start | bytes 1572868
  144.5 1.2 copy-start

commit v3 on v1

--- a/solution.py
+++ b/solution.py
@@ -20,7 +20,7 @@
     tok, cot, gate_w, up_w, down_w, gate_m, up_m, down_m,
     layer_out, token_grad, gate_g, up_g, down_g,
     feats, packed_0, packed_1, packed_2, meta, meta_sm, w_up, w_down, pre, act, psend, precv, hid, deltas,
-    tiles, gpack, gtransit, gfinal, gown, outs, ocore, oring, oyh, oyl,
+    tiles, gpack, gtransit, gfinal, gown, outs, ocore, oz_0, oz_1, oyh_0, oyh_1, oyl,
     yl_s, yl_r, yh_s, yh_r, z_s, z_r, c_s, c_r,
     ws_s, wf_s, w_r, meta_s, meta_r, meta_l, p_s, p_r,
     gt_s, gt_r, gf_s, gf_r, oc_s, oc_r, oz_s, oz_r, oyh_s, oyh_r, oyl_s, oyl_r,
@@ -35,7 +35,7 @@
 
     other_yl, other_yh, other_c = dev(flip_yl=True), dev(flip_yh=True), dev(flip_c=True)
     x_right, x_left, x_far = dev(dx=1), dev(dx=NX - 1), dev(dx=2)
-    z_next = (dev(dz=1), dev(dz=NZ - 1))
+    along_z = [dev(dz=k) for k in (1, 7, 2, 6, 3, 5, 4)]
 
     def remote(src, dst, send, recv, to):
         return pltpu.make_async_remote_copy(
@@ -54,7 +54,7 @@
         lax.fori_loop(0, n, step, 0)
 
     barrier = pltpu.get_barrier_semaphore()
-    partners = (other_yl, other_yh, other_c, x_right, x_left, x_far, *z_next)
+    partners = (other_yl, other_yh, other_c, x_right, x_left, x_far, *along_z)
     for to in partners:
         pl.semaphore_signal(barrier, inc=1, device_id=to, device_id_type=pl.DeviceIdType.MESH)
     pl.semaphore_wait(barrier, len(partners))
@@ -69,26 +69,39 @@
 
     home = chunk(yh, z, c)
 
-    def send_z(tc, at_z, w, e, hop):
-        q, h = chunk((yh + w) % 2, at_z, c), (yl + e) % 2
-        for d in range(2):
-            remote(feats.at[tc, q, h], feats.at[tc, q, h], z_s.at[d, hop - 1, tc, w, e], z_r.at[d, hop - 1, tc, w, e], z_next[d]).start()
-
-    def send_core(tc, at_z, w, e):
-        q, h = chunk((yh + w) % 2, at_z, c), (yl + e) % 2
-        remote(feats.at[tc, q, h], feats.at[tc, q, h], c_s.at[tc, q // 2, e], c_r.at[tc, q // 2, e], other_c).start()
-
-    def yh_piece(tc, e):
-        q, h = home, (yl + e) % 2
-        return remote(feats.at[tc, q, h], feats.at[tc, q, h], yh_s.at[tc, e], yh_r.at[tc, e], other_yh)
+    def homes(i):
+        return (z + jnp.where(i % 2 == 1, (i + 1) // 2, NZ - i // 2)) % NZ
+
+    def feature(tc, w, at_z, e):
+        return feats.at[tc, chunk((yh + w) % 2, at_z, c), (yl + e) % 2]
+
+    def send_core(tc, w, at_z, e):
+        piece, j = feature(tc, w, at_z, e), chunk((yh + w) % 2, at_z, c) // 2
+        remote(piece, piece, c_s.at[tc, j, e], c_r.at[tc, j, e], other_c).start()
+
+    def place(at_z):
+        return (at_z // 4) * 2 + at_z % 2
+
+    def send_yh(tc, at_z, e):
+        piece = feature(tc, 0, at_z, e)
+        remote(piece, piece, yh_s.at[tc, place(at_z), e], yh_r.at[tc, place(at_z), e], other_yh).start()
+
+    def from_yh(tc, at_z, e):
+        arrived(feature(tc, 1, at_z, e), yh_s.at[tc, place(at_z), e], yh_r.at[tc, place(at_z), e])
+
+    def send_z(tc, w, e):
+        piece, j = feature(tc, w, z, e), chunk((yh + w) % 2, z, c) // 2
+        for k in range(7):
+            remote(piece, piece, z_s.at[tc, w, e, k], z_r.at[tc, j, e], along_z[k]).start()
 
     def tokens_own(tc, ref):
         @pl.when(holder)
         def _():
             feats[tc, home, yl] = ref[...]
-            yh_piece(tc, 0).start()
-            send_z(tc, z, 0, 0, 1)
-            send_core(tc, z, 0, 0)
+            send_yh(tc, z, 0)
+            if tc == 0:
+                send_z(0, 0, 0)
+            send_core(tc, 0, z, 0)
 
         @pl.when(jnp.logical_not(holder))
         def _():
@@ -97,41 +110,45 @@
     def tokens_second(tc):
         @pl.when(holder)
         def _():
-            arrived(feats.at[tc, home, 1 - yl], yl_s.at[tc], yl_r.at[tc])
-            yh_piece(tc, 1).start()
-            send_z(tc, z, 0, 1, 1)
-            send_core(tc, z, 0, 1)
-
-    def tokens_third(tc):
+            arrived(feature(tc, 0, z, 1), yl_s.at[tc], yl_r.at[tc])
+            send_yh(tc, z, 1)
+            if tc == 1:
+                send_z(1, 0, 0)
+            send_z(tc, 0, 1)
+            send_core(tc, 0, z, 1)
+
+    def cotangents_third():
         @pl.when(holder)
         def _():
             for e in range(2):
-                arrived(feats.at[tc, chunk(1 - yh, z, c), (yl + e) % 2], yh_s.at[tc, e], yh_r.at[tc, e])
-                send_z(tc, z, 1, e, 1)
-                send_core(tc, z, 1, e)
-
-    def last_hop(d, w):
-        return jnp.where(w == d, 4, 3)
-
-    def tokens_hop(tc, hop):
+                from_yh(1, z, e)
+                send_z(1, 1, e)
+                send_core(1, 1, z, e)
+
+    def from_z(tc, w):
         def step(i):
-            w, e = i // 2, i % 2
-            for d in range(2):
-                at_z = (z + (NZ - hop if d == 0 else hop)) % NZ
-
-                @pl.when(jnp.logical_and(holds(at_z), hop <= last_hop(d, w)))
-                def _():
-                    q, h = chunk((yh + w) % 2, at_z, c), (yl + e) % 2
-                    piece = feats.at[tc, q, h]
-                    arrived(piece, z_s.at[d, hop - 1, tc, w, e], z_r.at[d, hop - 1, tc, w, e])
-
-                    @pl.when(hop < last_hop(d, w))
-                    def _():
-                        remote(piece, piece, z_s.at[d, hop, tc, w, e], z_r.at[d, hop, tc, w, e], z_next[d]).start()
-
-                    send_core(tc, at_z, w, e)
-
-        loop(4, step)
+            e, at_z = i // 7, homes(i % 7 + 1)
+
+            @pl.when(holds(at_z))
+            def _():
+                j = chunk((yh + w) % 2, at_z, c) // 2
+                arrived(feature(tc, w, at_z, e), z_s.at[tc, w, e, 0], z_r.at[tc, j, e])
+                if tc == 0:
+                    send_yh(0, at_z, e)
+                send_core(tc, w, at_z, e)
+
+        loop(14, step)
+
+    def tokens_from_yh():
+        def step(i):
+            e, at_z = i // 8, homes(i % 8)
+
+            @pl.when(holds(at_z))
+            def _():
+                from_yh(0, at_z, e)
+                send_core(0, 1, at_z, e)
+
+        loop(16, step)
 
     def tokens_from_core(tc):
         def step(i):
@@ -190,32 +207,29 @@
         loop(16, tile)
 
     tokens_own(0, tok)
-    for xx in range(NX):
-        for m in range(3):
-            packed[m][xx, SLOTS] = jnp.zeros((BLK, BLK), BF16)
+    tokens_own(1, cot)
     table = pack(0, jnp.zeros((8, BLK), jnp.int32))
-    tokens_own(1, cot)
     tokens_second(0)
     table = pack(1, table)
     table = pack(2, table)
     meta[x] = table
     for at, to in ((0, x_right), (1, x_left), (2, x_far)):
         remote(meta.at[x], meta.at[x], meta_s.at[at], meta_r.at[at], to).start()
-    tokens_third(0)
-    tokens_hop(0, 1)
     tokens_second(1)
-    tokens_hop(0, 2)
+    cotangents_third()
+    for xx in range(NX):
+        for m in range(3):
+            packed[m][xx, SLOTS] = jnp.zeros((BLK, BLK), BF16)
+    from_z(0, 0)
     forward_weights(0)
-    tokens_third(1)
-    tokens_hop(0, 3)
-    forward_weights(1)
     for at, origin in ((0, NX - 1), (1, 1), (2, 2)):
         arrived(meta.at[(x + origin) % NX], meta_s.at[at], meta_r.at[at])
     tables = pltpu.make_async_copy(meta, meta_sm, meta_l)
     tables.start()
-    tokens_hop(0, 4)
+    tokens_from_yh()
     tables.wait()
-    tokens_hop(1, 1)
+    unpack(0)
+    forward_weights(1)
 
     def features(tc, h):
         return jnp.concatenate([feats[tc, q, h] for q in range(16)], axis=1)
@@ -240,14 +254,12 @@
             arrived(precv.at[m, h], p_s.at[m, h], p_r.at[m, h])
 
     tokens_from_core(0)
-    unpack(0)
     exchange(0)
-    forward_weights(2)
-    tokens_hop(1, 2)
     unpack(1)
     exchange(1)
-    tokens_hop(1, 3)
-    tokens_hop(1, 4)
+    from_z(1, 0)
+    forward_weights(2)
+    from_z(1, 1)
     tokens_from_core(1)
     unpack(2)
     exchange(2)
@@ -290,8 +302,8 @@
 
     lows, highs = pl.ds(0, 4), pl.ds(4, 4)
 
-    def grad_send(m):
-        def part(i):
+    def grad_send(m, first=0, end=NX):
+        def part(i, carry):
             rel = (i + 2) % NX
             grad_partial(m, rel)
 
@@ -308,7 +320,9 @@
             def _():
                 remote(gpack.at[3, m, lows], gfinal.at[1, m, lows], gf_s.at[1, m, 0], gf_r.at[1, m, 0], x_left).start()
 
-        loop(NX, part)
+            return carry
+
+        lax.fori_loop(first, end, part, 0)
 
     def grad_transit(m):
         for at, rel, h, to in ((0, 1, 0, x_right), (1, 3, 1, x_left)):
@@ -329,9 +343,11 @@
             r, k = t // 4, t % 4
             out[r * BLK:(r + 1) * BLK, k * BLK:(k + 1) * BLK] = gown[m, meta_sm[x, m, t]]
 
-    def out_partial(o):
+    def out_partial(o, w):
+        at_yh = (yh + w) % 2
+
         def part(i):
-            xx, h = i // 2, i % 2
+            xx, h = at_yh * 2 + i // 2, i % 2
             if o == 0:
                 term = jnp.dot(hid[h], w_down[xx], preferred_element_type=F32)
             else:
@@ -343,67 +359,88 @@
             for k in range(4):
                 outs[o, xx * 4 + k, h] = term[:, k * BLK:(k + 1) * BLK]
 
-        loop(8, part)
-
-        def send(j):
-            remote(outs.at[o, j * 2 + 1 - c], ocore.at[o, j], oc_s.at[o, j], oc_r.at[o, j], other_c).start()
-
-        loop(8, send)
-
-    def out_core(o):
-        def step(j):
-            arrived(ocore.at[o, j], oc_s.at[o, j], oc_r.at[o, j])
-            q = j * 2 + c
-            outs[o, q] = (outs[o, q].astype(F32) + ocore[o, j].astype(F32)).astype(BF16)
+            @pl.when(h == 1)
+            def _():
+                for k in range(2):
+                    j = xx * 2 + k
+                    remote(outs.at[o, j * 2 + 1 - c], ocore.at[o, j], oc_s.at[o, j], oc_r.at[o, j], other_c).start()
+
+        loop(4, part)
+
+    def out_core(o, j):
+        arrived(ocore.at[o, j], oc_s.at[o, j], oc_r.at[o, j])
+        return outs[o, j * 2 + c].astype(F32) + ocore[o, j].astype(F32)
+
+    def to_home(o, j, dst, send, recv):
+        at_z = (j // 2) % 2 * 4 + yl * 2 + j % 2
+        q = j * 2 + c
+
+        @pl.when(at_z == z)
+        def _():
+            dst[...] = outs[o, q]
+
+        for k, dz in enumerate((1, 7, 2, 6, 3, 5, 4)):
+
+            @pl.when(at_z == (z + dz) % NZ)
+            def _():
+                remote(outs.at[o, q], dst, send, recv, along_z[k]).start()
+
+    def layer_out_to_homes():
+        def step(i):
+            j = (i // 4 + yh + 1) % 2 * 4 + i % 4
+            outs[0, j * 2 + c] = out_core(0, j).astype(BF16)
+            to_home(0, j, oz_0.at[j // 4, z], oz_s.at[0, j], oz_r.at[0, j // 4, z])
 
         loop(8, step)
 
-    def out_hop(o, hop):
+    def token_grad_to_yh():
         def step(i):
-            w, h = i // 2, i % 2
-            for d in range(2):
-                at_z = (z + (hop if d == 0 else NZ - hop)) % NZ
-
-                @pl.when(jnp.logical_and(holds(at_z), hop <= last_hop(d, w)))
-                def _():
-                    q = chunk((yh + w) % 2, at_z, c)
-                    j = q // 2
-
-                    @pl.when(hop < last_hop(d, w))
-                    def _():
-                        arrived(oring.at[d, o, j, h], oz_s.at[o, j, h], oz_r.at[d, o, j, h])
-                        outs[o, q, h] = (outs[o, q, h].astype(F32) + oring[d, o, j, h].astype(F32)).astype(BF16)
-
-                    remote(outs.at[o, q, h], oring.at[d, o, j, h], oz_s.at[o, j, h], oz_r.at[d, o, j, h], z_next[d]).start()
+            j = (1 - yh) * 4 + i
+            outs[1, j * 2 + c] = out_core(1, j).astype(BF16)
+            remote(outs.at[1, j * 2 + c], oyh_1.at[i], oyh_s.at[1, i], oyh_r.at[1, i], other_yh).start()
 
         loop(4, step)
 
-    def out_home(o):
+    def token_grad_to_homes():
+        def step(i):
+            j = yh * 4 + i
+            total = out_core(1, j)
+            arrived(oyh_1.at[i], oyh_s.at[1, i], oyh_r.at[1, i])
+            outs[1, j * 2 + c] = (total + oyh_1[i].astype(F32)).astype(BF16)
+            to_home(1, j, oz_1.at[z], oz_s.at[1, j], oz_r.at[1, 0, z])
+
+        loop(4, step)
+
+    def at_home(o, at_yh):
+        def wait(i):
+            at_z = homes(i + 1)
+            dst = oz_0.at[at_yh, at_z] if o == 0 else oz_1.at[at_z]
+            arrived(dst, oz_s.at[o, 0], oz_r.at[o, at_yh if o == 0 else 0, at_z])
+
+        loop(7, wait)
+        terms = oz_0.at[at_yh] if o == 0 else oz_1
+        total = terms[0].astype(F32)
+        for k in range(1, NZ):
+            total += terms[k].astype(F32)
+        return total
+
+    def layer_out_yh():
         @pl.when(holder)
         def _():
-            for w in (1, 0):
-                for h in range(2):
-                    q = chunk((yh + w) % 2, z, c)
-                    j = q // 2
-                    for d in range(2):
-                        arrived(oring.at[d, o, j, h], oz_s.at[o, j, h], oz_r.at[d, o, j, h])
-                    total = outs[o, q, h].astype(F32) + oring[0, o, j, h].astype(F32) + oring[1, o, j, h].astype(F32)
-                    outs[o, q, h] = total.astype(BF16)
-                    if w == 1:
-                        remote(outs.at[o, q, h], oyh.at[o, h], oyh_s.at[o, h], oyh_r.at[o, h], other_yh).start()
+            q = chunk(1 - yh, z, c)
+            outs[0, q] = at_home(0, 1 - yh).astype(BF16)
+            remote(outs.at[0, q], oyh_0, oyh_s.at[0, 0], oyh_r.at[0, 0], other_yh).start()
 
     def out_last(o, out):
         @pl.when(holder)
         def _():
-            for e in (1, 0):
-                h = (yl + e) % 2
-                arrived(oyh.at[o, h], oyh_s.at[o, h], oyh_r.at[o, h])
-                total = (outs[o, home, h].astype(F32) + oyh[o, h].astype(F32)).astype(BF16)
-                if e == 1:
-                    outs[o, home, h] = total
-                    remote(outs.at[o, home, h], oyl.at[o], oyl_s.at[o], oyl_r.at[o], other_yl).start()
-                else:
-                    out[...] = total
+            total = at_home(o, yh)
+            if o == 0:
+                arrived(oyh_0, oyh_s.at[0, 0], oyh_r.at[0, 0])
+                total += oyh_0[...].astype(F32)
+            outs[o, home] = total.astype(BF16)
+            remote(outs.at[o, home, 1 - yl], oyl.at[o], oyl_s.at[o], oyl_r.at[o], other_yl).start()
+            out[...] = outs[o, home, yl]
 
     def out_other(o, out):
         @pl.when(jnp.logical_not(holder))
@@ -411,12 +448,12 @@
             arrived(oyl.at[o], oyl_s.at[o], oyl_r.at[o])
             out[...] = oyl[o]
 
-    grad_send(2)
-    out_partial(0)
+    grad_send(2, 0, 1)
+    out_partial(0, 1)
+    out_partial(0, 0)
+    grad_send(2, 1)
+    layer_out_to_homes()
     grad_transit(2)
-    out_core(0)
-    out_hop(0, 4)
-    out_hop(0, 3)
     exchanged(2)
 
     def delta(i):
@@ -426,80 +463,80 @@
         deltas[1, h, rows, :] = (hg * act[1, h, rows, :]).astype(BF16)
 
     loop(8, delta)
-    grad_send(0)
-    out_hop(0, 2)
-    grad_send(1)
-    out_hop(0, 1)
+    grad_send(0, 0, 1)
+    out_partial(1, 1)
+    out_partial(1, 0)
+    grad_send(0, 1, 2)
+    token_grad_to_yh()
+    grad_send(0, 2)
+    grad_send(1, 0, 1)
     grad_transit(0)
-    out_partial(1)
+    token_grad_to_homes()
+    grad_send(1, 1)
     grad_transit(1)
-    out_core(1)
-    out_hop(1, 4)
-    out_home(0)
-    out_hop(1, 3)
+    layer_out_yh()
+    out_last(0, layer_out)
+    out_last(1, token_grad)
     grad_finish(2, down_g)
-    out_hop(1, 2)
-    out_last(0, layer_out)
-    out_hop(1, 1)
-    out_home(1)
     grad_finish(0, gate_g)
     grad_finish(1, up_g)
-    out_last(1, token_grad)
     out_other(0, layer_out)
     out_other(1, token_grad)
 
     def left(src, send):
-        remote(src, src, send, z_r.at[0, 0, 0, 0, 0], other_c).wait_send()
-
-    piece = feats.at[0, 0, 0]
-    for tc in range(2):
-
-        @pl.when(holder)
-        def _():
-            for e in range(2):
-                left(piece, yh_s.at[tc, e])
-
-                for w in range(2):
-                    for d in range(2):
-                        left(piece, z_s.at[d, 0, tc, w, e])
-
-        @pl.when(jnp.logical_not(holder))
-        def _():
+        remote(src, src, send, z_r.at[0, 0, 0], other_c).wait_send()
+
+    piece, rows = feats.at[0, 0, 0], ocore.at[0, 0]
+
+    def tokens_left(i):
+        e, at_z = i // 8, homes(i % 8)
+
+        @pl.when(holds(at_z))
+        def _():
+            left(piece, yh_s.at[0, place(at_z), e])
+
+        j = i // 2
+        for tc in range(2):
+            left(piece, c_s.at[tc, j, i % 2])
+
+        @pl.when(jnp.logical_not(jnp.logical_and(holder, (j // 2) % 2 * 4 + yl * 2 + j % 2 == z)))
+        def _():
+            @pl.when(i % 2 == 0)
+            def _():
+                left(rows, oz_s.at[0, j])
+
+                @pl.when(j // 4 == yh)
+                def _():
+                    left(rows, oz_s.at[1, j])
+
+        for o in range(2):
+
+            @pl.when(i % 2 == o)
+            def _():
+                left(rows, oc_s.at[o, j])
+
+    loop(16, tokens_left)
+
+    def z_left(k):
+        for e in range(2):
+            for tc, w in ((0, 0), (1, 0), (1, 1)):
+                left(piece, z_s.at[tc, w, e, k])
+
+    for i in range(4):
+        left(rows, oyh_s.at[1, i])
+
+    @pl.when(holder)
+    def _():
+        loop(7, z_left)
+        left(rows, oyh_s.at[0, 0])
+        for o in range(2):
+            left(piece, yh_s.at[1, place(z), o])
+            left(piece, oyl_s.at[o])
+
+    @pl.when(jnp.logical_not(holder))
+    def _():
+        for tc in range(2):
             left(piece, yl_s.at[tc])
-
-        def hops(i):
-            w, e = i // 2, i % 2
-            for hop in range(1, 4):
-                for d in range(2):
-                    at_z = (z + (NZ - hop if d == 0 else hop)) % NZ
-
-                    @pl.when(jnp.logical_and(holds(at_z), hop < last_hop(d, w)))
-                    def _():
-                        left(piece, z_s.at[d, hop, tc, w, e])
-
-        loop(4, hops)
-
-        def cores(i):
-            left(piece, c_s.at[tc, i // 2, i % 2])
-
-        loop(16, cores)
-        o = tc
-
-        def ocores(j):
-            left(ocore.at[0, 0], oc_s.at[o, j])
-
-            @pl.when(jnp.logical_not(jnp.logical_and(holder, jnp.logical_and((j // 2) % 2 == z // 4, j % 2 == z % 2))))
-            def _():
-                for h in range(2):
-                    left(piece, oz_s.at[o, j, h])
-
-        loop(8, ocores)
-
-        @pl.when(holder)
-        def _():
-            for h in range(2):
-                left(piece, oyh_s.at[o, h])
-            left(piece, oyl_s.at[o])
 
     half = gtransit.at[0, 0]
     for at in range(3):
@@ -543,19 +580,21 @@
             pltpu.VMEM((3, SLOTS + 1, BLK, BLK), BF16),
             pltpu.VMEM((2, 16, 2, 256, BLK), BF16),
             pltpu.VMEM((2, 8, 2, 256, BLK), BF16),
-            pltpu.VMEM((2, 2, 8, 2, 256, BLK), BF16),
-            pltpu.VMEM((2, 2, 256, BLK), BF16),
+            pltpu.VMEM((2, NZ, 2, 256, BLK), BF16),
+            pltpu.VMEM((NZ, 2, 256, BLK), BF16),
             pltpu.VMEM((2, 256, BLK), BF16),
-            dma((2,)), dma((2,)), dma((2, 2)), dma((2, 2)),
-            dma((2, 4, 2, 2, 2)), dma((2, 4, 2, 2, 2)),
+            pltpu.VMEM((4, 2, 256, BLK), BF16),
+            pltpu.VMEM((2, 256, BLK), BF16),
+            dma((2,)), dma((2,)), dma((2, 4, 2)), dma((2, 4, 2)),
+            dma((2, 2, 2, 7)), dma((2, 8, 2)),
             dma((2, 8, 2)), dma((2, 8, 2)),
             dma((2, 3, 2)), dma((3, 2)), dma((3, 3, 2)),
             dma((3,)), dma((3,)), dma(()),
             dma((3, 2)), dma((3, 2)),
             dma((2, 3)), dma((2, 3)), dma((2, 3, 2)), dma((2, 3, 2)),
             dma((2, 8)), dma((2, 8)),
-            dma((2, 8, 2)), dma((2, 2, 8, 2)),
-            dma((2, 2)), dma((2, 2)), dma((2,)), dma((2,)),
+            dma((2, 8)), dma((2, 2, NZ)),
+            dma((2, 4)), dma((2, 4)), dma((2,)), dma((2,)),
         ],
         compiler_params=pltpu.CompilerParams(
             collective_id=0, has_side_effects=True, vmem_limit_bytes=58 * 2**20

time: 130 us -> 146 us (1.12)
  Pallas kernels: 123 us -> 138 us
    pallas_call x1, Pallas kernels: 123 us -> 138 us  [body(): pl.pallas_call(kernel, out_shape=tuple((jax.ShapeDtypeStruct(a.shape, a.d...]
where the time goes in v3:
time: 146 us; the launch traced here: 145 us
  Pallas kernels  138 us (95%)
  local copies, waits for them, and re-layouts  6.09 us (4%)
    pallas_call x1, Pallas kernels, body(): pl.pallas_call(kernel, out_shape=tuple((jax.ShapeDtypeStruct(a.shape, a.d...  138 us
    unnamed x11, local copies, waits for them, and re-layouts  6.09 us

profile of v3, /device:TPU:8, one launch (start us, length us, event | category | flops | bytes accessed | tf_op | source)
XLA Modules:
  0.0 144.5 jit_solution(18438373581225300212)
XLA Ops:
  0.6 137.8 %shard_map.119 = (bf16[256,128]{1,0:T(8,128)(2,1)}, bf16[256,128]{1,0:T(8,128)(2,1)}, bf16[512,512]{1,0:T(8,128)(2,1)}, bf16[512,512]{1,0:T(8,128)(2,1)}, bf16[512,512]{1,0:T(8,128)(2,1)}) custom-call(bf16[256,128]{1,0:T(8,128)(2,1)} %tok.1, bf16[256,128]{1,0:T(8,128)(2,1)} %cot.1, bf16[512,512]{1,0:T(8,128)(2,1)} %gate_w.1, bf16[512,512]{1,0:T(8,128)(2,1)} %up_w.1, ...), custom_call_target="tpu_custom_call" | custom-call | flops 9663676416 | bytes 4194304 | tf_op jit(solution)/shard_map/pallas_call | solution.py:558
  138.4 0.0 copy-start.2
  138.4 1.5 %copy.18 = bf16[256,128]{1,0:T(8,128)(2,1)} copy(bf16[256,128]{1,0:T(8,128)(2,1)} %get-tuple-element.10) | data formatting | bytes 131072
  140.0 0.0 copy-done.2
  140.0 0.6 copy.19
  140.6 0.0 copy-start.1
  140.6 1.9 %copy.20 = bf16[512,512]{1,0:T(8,128)(2,1)} copy(bf16[512,512]{1,0:T(8,128)(2,1)} %get-tuple-element.12) | data formatting | bytes 1048576
  142.5 0.0 copy-done.1
  142.5 0.0 copy-start
  142.5 0.8 copy.21
  143.3 0.4 copy-done
  143.7 0.8 copy.22
Async XLA Ops:
  138.4 1.5 %copy-start.2 = (bf16[256,128]{1,0:T(8,128)(2,1)S(1)}, bf16[256,128]{1,0:T(8,128)(2,1)}, u32[]{:S(2)}) copy-start(bf16[256,128]{1,0:T(8,128)(2,1)} %get-tuple-element.11) | copy-start | bytes 196612
  140.6 1.9 %copy-start.1 = (bf16[512,512]{1,0:T(8,128)(2,1)S(1)}, bf16[512,512]{1,0:T(8,128)(2,1)}, u32[]{:S(2)}) copy-start(bf16[512,512]{1,0:T(8,128)(2,1)} %get-tuple-element.13) | copy-start | bytes 1572868
  142.5 1.2 copy-start

commit v4 on v3

--- a/solution.py
+++ b/solution.py
@@ -18,12 +18,12 @@
 
 def kernel(
     tok, cot, gate_w, up_w, down_w, gate_m, up_m, down_m,
-    layer_out, token_grad, gate_g, up_g, down_g,
+    layer_out, token_grad, gown,
     feats, packed_0, packed_1, packed_2, meta, meta_sm, w_up, w_down, pre, act, psend, precv, hid, deltas,
-    tiles, gpack, gtransit, gfinal, gown, outs, ocore, oz_0, oz_1, oyh_0, oyh_1, oyl,
-    yl_s, yl_r, yh_s, yh_r, z_s, z_r, c_s, c_r,
+    tiles, gpack, gtransit, gfinal, outs, ocore, oz_0, oz_1, oleaf, oyh_0, oyh_1, oyl,
+    yl_s, yl_r, yh_s, yh_r, z_s, z_r, zf_s, zd_s, c_s, c_r,
     ws_s, wf_s, w_r, meta_s, meta_r, meta_l, p_s, p_r,
-    gt_s, gt_r, gf_s, gf_r, oc_s, oc_r, oz_s, oz_r, oyh_s, oyh_r, oyl_s, oyl_r,
+    gt_s, gt_r, gf_s, gf_r, oc_s, oc_r, oz_s, oz_r, ol_r, oyh_s, oyh_r, oyl_s, oyl_r,
 ):
     dp, mp = lax.axis_index("dp"), lax.axis_index("mp")
     x, yl = dp // 2, dp % 2
@@ -36,6 +36,7 @@
     other_yl, other_yh, other_c = dev(flip_yl=True), dev(flip_yh=True), dev(flip_c=True)
     x_right, x_left, x_far = dev(dx=1), dev(dx=NX - 1), dev(dx=2)
     along_z = [dev(dz=k) for k in (1, 7, 2, 6, 3, 5, 4)]
+    z_next = along_z[:2]
 
     def remote(src, dst, send, recv, to):
         return pltpu.make_async_remote_copy(
@@ -89,19 +90,24 @@
     def from_yh(tc, at_z, e):
         arrived(feature(tc, 1, at_z, e), yh_s.at[tc, place(at_z), e], yh_r.at[tc, place(at_z), e])
 
+    def steps(e, k):
+        return (k if e == 0 else NZ - k) % NZ
+
     def send_z(tc, w, e):
         piece, j = feature(tc, w, z, e), chunk((yh + w) % 2, z, c) // 2
-        for k in range(7):
-            remote(piece, piece, z_s.at[tc, w, e, k], z_r.at[tc, j, e], along_z[k]).start()
+        for d in range(2):
+            remote(piece, piece, z_s.at[tc, w, e, d], z_r.at[tc, j, e], z_next[d]).start()
 
     def tokens_own(tc, ref):
         @pl.when(holder)
         def _():
             feats[tc, home, yl] = ref[...]
             send_yh(tc, z, 0)
+            send_core(tc, 0, z, 0)
             if tc == 0:
-                send_z(0, 0, 0)
-            send_core(tc, 0, z, 0)
+                for k in range(7):
+                    piece = feature(0, 0, z, 0)
+                    remote(piece, piece, zd_s.at[k], z_r.at[0, home // 2, 0], along_z[6 - k]).start()
 
         @pl.when(jnp.logical_not(holder))
         def _():
@@ -112,50 +118,69 @@
         def _():
             arrived(feature(tc, 0, z, 1), yl_s.at[tc], yl_r.at[tc])
             send_yh(tc, z, 1)
-            if tc == 1:
-                send_z(1, 0, 0)
-            send_z(tc, 0, 1)
+            if tc == 0:
+                send_z(0, 0, 1)
             send_core(tc, 0, z, 1)
 
     def cotangents_third():
         @pl.when(holder)
         def _():
+            for e in range(2):
+                send_z(1, 0, e)
             for e in range(2):
                 from_yh(1, z, e)
                 send_z(1, 1, e)
                 send_core(1, 1, z, e)
 
-    def from_z(tc, w):
+    def tokens_first():
         def step(i):
-            e, at_z = i // 7, homes(i % 7 + 1)
+            at_z = homes(i + 1)
 
             @pl.when(holds(at_z))
             def _():
-                j = chunk((yh + w) % 2, at_z, c) // 2
-                arrived(feature(tc, w, at_z, e), z_s.at[tc, w, e, 0], z_r.at[tc, j, e])
-                if tc == 0:
-                    send_yh(0, at_z, e)
-                send_core(tc, w, at_z, e)
-
-        loop(14, step)
-
-    def tokens_from_yh():
-        def step(i):
-            e, at_z = i // 8, homes(i % 8)
+                arrived(feature(0, 0, at_z, 0), zd_s.at[0], z_r.at[0, chunk(yh, at_z, c) // 2, 0])
+                send_yh(0, at_z, 0)
+                send_core(0, 0, at_z, 0)
+
+        loop(7, step)
+
+    def z_hop(tc, hop):
+        for w in range(1 + tc):
+            for e in range(1 - tc, 2):
+                for d in range(2):
+                    last = 4 if e == d else 3
+                    if hop > last:
+                        continue
+                    at_z = (z + (NZ - hop if d == 0 else hop)) % NZ
+
+                    @pl.when(holds(at_z))
+                    def _():
+                        piece, j = feature(tc, w, at_z, e), chunk((yh + w) % 2, at_z, c) // 2
+                        arrived(piece, zf_s.at[tc, j, e], z_r.at[tc, j, e])
+                        if hop < last:
+                            remote(piece, piece, zf_s.at[tc, j, e], z_r.at[tc, j, e], z_next[d]).start()
+                        if tc == 0:
+                            send_yh(0, at_z, e)
+                        send_core(tc, w, at_z, e)
+
+    def tokens_from_yh(e, first, end):
+        def step(i, carry):
+            at_z = homes(i)
 
             @pl.when(holds(at_z))
             def _():
                 from_yh(0, at_z, e)
                 send_core(0, 1, at_z, e)
 
-        loop(16, step)
-
-    def tokens_from_core(tc):
-        def step(i):
-            j, e = i // 2, i % 2
+            return carry
+
+        lax.fori_loop(first, end, step, 0)
+
+    def tokens_from_core(tc, e):
+        def step(j):
             arrived(feats.at[tc, j * 2 + 1 - c, (yl + e) % 2], c_s.at[tc, j, e], c_r.at[tc, j, e])
 
-        loop(16, step)
+        loop(8, step)
 
     packed = (packed_0, packed_1, packed_2)
     masks, weights = (gate_m, up_m, down_m), (gate_w, up_w, down_w)
@@ -176,11 +201,13 @@
         for s in range(SLOTS):
             table = jnp.where(lane == m * BLK + TILES + s, ids[s], table)
             packed[m][x, s] = tiles[ids[s]]
+        return table
+
+    def send_weights(m, part):
         for at, to in ((0, x_right), (1, x_left)):
-            for h in range(2):
-                half = packed[m].at[x, pl.ds(h * 4, 4)]
-                remote(half, half, ws_s.at[at, m, h], w_r.at[at, m, h], to).start()
-        return table
+            h = (at + part) % 2
+            half = packed[m].at[x, pl.ds(h * 4, 4)]
+            remote(half, half, ws_s.at[at, m, h], w_r.at[at, m, h], to).start()
 
     def forward_weights(m):
         for at, h, origin, to in ((0, 0, NX - 1, x_right), (1, 1, 1, x_left)):
@@ -209,33 +236,43 @@
     tokens_own(0, tok)
     tokens_own(1, cot)
     table = pack(0, jnp.zeros((8, BLK), jnp.int32))
+    send_weights(0, 0)
+    send_weights(0, 1)
     tokens_second(0)
     table = pack(1, table)
+    send_weights(1, 0)
     table = pack(2, table)
     meta[x] = table
     for at, to in ((0, x_right), (1, x_left), (2, x_far)):
         remote(meta.at[x], meta.at[x], meta_s.at[at], meta_r.at[at], to).start()
-    tokens_second(1)
-    cotangents_third()
     for xx in range(NX):
         for m in range(3):
             packed[m][xx, SLOTS] = jnp.zeros((BLK, BLK), BF16)
-    from_z(0, 0)
+    tokens_second(1)
     forward_weights(0)
+    send_weights(1, 1)
+    send_weights(2, 0)
+    tokens_first()
+    cotangents_third()
+    z_hop(0, 1)
+    forward_weights(1)
+    send_weights(2, 1)
+    tokens_from_yh(0, 0, 8)
+    z_hop(0, 2)
+    z_hop(1, 1)
     for at, origin in ((0, NX - 1), (1, 1), (2, 2)):
         arrived(meta.at[(x + origin) % NX], meta_s.at[at], meta_r.at[at])
     tables = pltpu.make_async_copy(meta, meta_sm, meta_l)
     tables.start()
-    tokens_from_yh()
     tables.wait()
     unpack(0)
-    forward_weights(1)
 
     def features(tc, h):
         return jnp.concatenate([feats[tc, q, h] for q in range(16)], axis=1)
 
-    def exchange(m):
-        def rows(h):
+    def exchange(m, e):
+        def rows(i):
+            h = (yl + e) % 2
             if m < 2:
                 total = jnp.dot(features(0, h), w_up[m], preferred_element_type=F32)
             else:
@@ -247,37 +284,54 @@
             psend[m, h] = total.astype(BF16)
             remote(psend.at[m, h], precv.at[m, h], p_s.at[m, h], p_r.at[m, h], other_yl).start()
 
-        loop(2, rows)
-
-    def exchanged(m):
-        for h in range(2):
-            arrived(precv.at[m, h], p_s.at[m, h], p_r.at[m, h])
-
-    tokens_from_core(0)
-    exchange(0)
+        rows(0)
+
+    def exchanged(m, e):
+        h = (yl + e) % 2
+        arrived(precv.at[m, h], p_s.at[m, h], p_r.at[m, h])
+
+    tokens_from_core(0, 0)
+    exchange(0, 0)
+    z_hop(0, 3)
+    z_hop(1, 2)
+    forward_weights(2)
+    z_hop(0, 4)
     unpack(1)
-    exchange(1)
-    from_z(1, 0)
-    forward_weights(2)
-    from_z(1, 1)
-    tokens_from_core(1)
-    unpack(2)
-    exchange(2)
-
-    exchanged(0)
-    exchanged(1)
-
-    def activate(i):
-        h, rows = i // 4, pl.ds(pl.multiple_of((i % 4) * 64, 64), 64)
-        g = pre[0, h, rows, :] + precv[0, h, rows, :].astype(F32)
-        u = pre[1, h, rows, :] + precv[1, h, rows, :].astype(F32)
-        sigmoid = 1.0 / (1.0 + jnp.exp(-g))
-        activated = g * sigmoid
-        hid[h, rows, :] = (activated * u).astype(BF16)
-        act[0, h, rows, :] = u * sigmoid * (1.0 + g * (1.0 - sigmoid))
-        act[1, h, rows, :] = activated
-
-    loop(8, activate)
+    exchange(1, 0)
+    z_hop(1, 3)
+    tokens_from_yh(1, 0, 8)
+    z_hop(1, 4)
+    tokens_from_core(0, 1)
+    exchange(0, 1)
+    exchange(1, 1)
+    def activate(e):
+        h = (yl + e) % 2
+
+        def part(i):
+            rows = pl.ds(pl.multiple_of(i * 64, 64), 64)
+            g = pre[0, h, rows, :] + precv[0, h, rows, :].astype(F32)
+            u = pre[1, h, rows, :] + precv[1, h, rows, :].astype(F32)
+            sigmoid = 1.0 / (1.0 + jnp.exp(-g))
+            activated = g * sigmoid
+            hid[h, rows, :] = (activated * u).astype(BF16)
+            act[0, h, rows, :] = u * sigmoid * (1.0 + g * (1.0 - sigmoid))
+            act[1, h, rows, :] = activated
+
+        exchanged(0, e)
+        exchanged(1, e)
+        loop(4, part)
+
+    def delta(e):
+        h = (yl + e) % 2
+
+        def part(i):
+            rows = pl.ds(pl.multiple_of(i * 64, 64), 64)
+            hg = pre[2, h, rows, :] + precv[2, h, rows, :].astype(F32)
+            deltas[0, h, rows, :] = (hg * act[0, h, rows, :]).astype(BF16)
+            deltas[1, h, rows, :] = (hg * act[1, h, rows, :]).astype(BF16)
+
+        exchanged(2, e)
+        loop(4, part)
 
     contract_rows = (((0,), (0,)), ((), ()))
 
@@ -331,23 +385,20 @@
             gpack[rel, m, part] = (gpack[rel, m, part].astype(F32) + gtransit[at, m].astype(F32)).astype(BF16)
             remote(gpack.at[rel, m, part], gfinal.at[at, m, part], gf_s.at[at, m, h], gf_r.at[at, m, h], to).start()
 
-    def grad_finish(m, out):
+    def grad_finish(m):
         for at in range(2):
             for h in range(2):
                 arrived(gfinal.at[at, m, pl.ds(h * 4, 4)], gf_s.at[at, m, h], gf_r.at[at, m, h])
-        for s in range(SLOTS):
-            total = gpack[0, m, s].astype(F32) + gfinal[0, m, s].astype(F32) + gfinal[1, m, s].astype(F32)
-            gown[m, s] = (total * SCALE).astype(BF16)
+        for i in range(SLOTS):
+            total = gpack[0, m, i].astype(F32) + gfinal[0, m, i].astype(F32) + gfinal[1, m, i].astype(F32)
+            gown[m, i] = (total * SCALE).astype(BF16)
         gown[m, SLOTS] = jnp.zeros((BLK, BLK), BF16)
-        for t in range(TILES):
-            r, k = t // 4, t % 4
-            out[r * BLK:(r + 1) * BLK, k * BLK:(k + 1) * BLK] = gown[m, meta_sm[x, m, t]]
-
-    def out_partial(o, w):
-        at_yh = (yh + w) % 2
+
+    def out_partial(o, w, e):
+        at_yh, h = (yh + w) % 2, (yl + e) % 2
 
         def part(i):
-            xx, h = at_yh * 2 + i // 2, i % 2
+            xx = at_yh * 2 + i
             if o == 0:
                 term = jnp.dot(hid[h], w_down[xx], preferred_element_type=F32)
             else:
@@ -358,70 +409,104 @@
             term = term.astype(BF16)
             for k in range(4):
                 outs[o, xx * 4 + k, h] = term[:, k * BLK:(k + 1) * BLK]
-
-            @pl.when(h == 1)
+            for k in range(2):
+                j = xx * 2 + k
+                remote(outs.at[o, j * 2 + 1 - c, h], ocore.at[o, j, h], oc_s.at[o, j, h], oc_r.at[o, j, h], other_c).start()
+
+        loop(2, part)
+
+    def out_core(o, j, h):
+        arrived(ocore.at[o, j, h], oc_s.at[o, j, h], oc_r.at[o, j, h])
+        return outs[o, j * 2 + c, h].astype(F32) + ocore[o, j, h].astype(F32)
+
+    def far(j, h):
+        up = (z - ((j // 2) % 2 * 4 + yl * 2 + j % 2) + NZ) % NZ
+        return jnp.where(h == 0, up, (NZ - up) % NZ)
+
+    def on(h, k):
+        return dev(dz=jnp.where(h == 0, k, NZ - k) % NZ)
+
+    def to_home(o, j, h, k):
+        slot = (1, 3, 6, 7).index(k)
+        dst = oz_0.at[j // 4, slot, h] if o == 0 else oz_1.at[slot, h]
+        recv = oz_r.at[o, j // 4 if o == 0 else 0, slot, h]
+        remote(outs.at[o, j * 2 + c, h], dst, oz_s.at[o, j, h], recv, on(h, NZ - k)).start()
+
+    def leaf(o, j, h):
+        k = far(j, h)
+
+        @pl.when(k == 7)
+        def _():
+            to_home(o, j, h, 7)
+
+        @pl.when(jnp.logical_or(k == 5, jnp.logical_or(k == 4, k == 2)))
+        def _():
+            to = on(h, jnp.where(k == 5, 1, 7))
+            remote(outs.at[o, j * 2 + c, h], oleaf.at[o, j, h], oz_s.at[o, j, h], ol_r.at[o, j, h], to).start()
+
+    def relays(o, e):
+        h = (yl + e) % 2
+
+        def step(i):
+            j = i if o == 0 else yh * 4 + i
+            k, q = far(j, h), j * 2 + c
+
+            @pl.when(jnp.logical_or(k == 6, jnp.logical_or(k == 3, k == 1)))
             def _():
-                for k in range(2):
-                    j = xx * 2 + k
-                    remote(outs.at[o, j * 2 + 1 - c], ocore.at[o, j], oc_s.at[o, j], oc_r.at[o, j], other_c).start()
-
-        loop(4, part)
-
-    def out_core(o, j):
-        arrived(ocore.at[o, j], oc_s.at[o, j], oc_r.at[o, j])
-        return outs[o, j * 2 + c].astype(F32) + ocore[o, j].astype(F32)
-
-    def to_home(o, j, dst, send, recv):
-        at_z = (j // 2) % 2 * 4 + yl * 2 + j % 2
-        q = j * 2 + c
-
-        @pl.when(at_z == z)
-        def _():
-            dst[...] = outs[o, q]
-
-        for k, dz in enumerate((1, 7, 2, 6, 3, 5, 4)):
-
-            @pl.when(at_z == (z + dz) % NZ)
-            def _():
-                remote(outs.at[o, q], dst, send, recv, along_z[k]).start()
-
-    def layer_out_to_homes():
+                arrived(oleaf.at[o, j, h], oz_s.at[o, j, h], ol_r.at[o, j, h])
+                outs[o, q, h] = (outs[o, q, h].astype(F32) + oleaf[o, j, h].astype(F32)).astype(BF16)
+                for at in (1, 3, 6):
+
+                    @pl.when(k == at)
+                    def _():
+                        to_home(o, j, h, at)
+
+        loop(8 if o == 0 else 4, step)
+
+    def layer_out_leaves(e):
+        h = (yl + e) % 2
+
         def step(i):
             j = (i // 4 + yh + 1) % 2 * 4 + i % 4
-            outs[0, j * 2 + c] = out_core(0, j).astype(BF16)
-            to_home(0, j, oz_0.at[j // 4, z], oz_s.at[0, j], oz_r.at[0, j // 4, z])
+            outs[0, j * 2 + c, h] = out_core(0, j, h).astype(BF16)
+            leaf(0, j, h)
 
         loop(8, step)
 
-    def token_grad_to_yh():
+    def token_grad_to_yh(e):
+        h = (yl + e) % 2
+
         def step(i):
             j = (1 - yh) * 4 + i
-            outs[1, j * 2 + c] = out_core(1, j).astype(BF16)
-            remote(outs.at[1, j * 2 + c], oyh_1.at[i], oyh_s.at[1, i], oyh_r.at[1, i], other_yh).start()
+            q = j * 2 + c
+            outs[1, q, h] = out_core(1, j, h).astype(BF16)
+            remote(outs.at[1, q, h], oyh_1.at[i, h], oyh_s.at[1, i, h], oyh_r.at[1, i, h], other_yh).start()
 
         loop(4, step)
 
-    def token_grad_to_homes():
+    def token_grad_leaves(e):
+        h = (yl + e) % 2
+
         def step(i):
             j = yh * 4 + i
-            total = out_core(1, j)
-            arrived(oyh_1.at[i], oyh_s.at[1, i], oyh_r.at[1, i])
-            outs[1, j * 2 + c] = (total + oyh_1[i].astype(F32)).astype(BF16)
-            to_home(1, j, oz_1.at[z], oz_s.at[1, j], oz_r.at[1, 0, z])
+            total = out_core(1, j, h)
+            arrived(oyh_1.at[i, h], oyh_s.at[1, i, h], oyh_r.at[1, i, h])
+            outs[1, j * 2 + c, h] = (total + oyh_1[i, h].astype(F32)).astype(BF16)
+            leaf(1, j, h)
 
         loop(4, step)
 
     def at_home(o, at_yh):
+        terms = oz_0.at[at_yh] if o == 0 else oz_1
+
         def wait(i):
-            at_z = homes(i + 1)
-            dst = oz_0.at[at_yh, at_z] if o == 0 else oz_1.at[at_z]
-            arrived(dst, oz_s.at[o, 0], oz_r.at[o, at_yh if o == 0 else 0, at_z])
-
-        loop(7, wait)
-        terms = oz_0.at[at_yh] if o == 0 else oz_1
-        total = terms[0].astype(F32)
-        for k in range(1, NZ):
-            total += terms[k].astype(F32)
+            slot, h = i // 2, i % 2
+            arrived(terms.at[slot, h], oz_s.at[o, 0, h], oz_r.at[o, at_yh if o == 0 else 0, slot, h])
+
+        loop(8, wait)
+        total = outs[o, chunk(at_yh, z, c)].astype(F32)
+        for slot in range(4):
+            total += terms[slot].astype(F32)
         return total
 
     def layer_out_yh():
@@ -429,14 +514,14 @@
         def _():
             q = chunk(1 - yh, z, c)
             outs[0, q] = at_home(0, 1 - yh).astype(BF16)
-            remote(outs.at[0, q], oyh_0, oyh_s.at[0, 0], oyh_r.at[0, 0], other_yh).start()
+            remote(outs.at[0, q], oyh_0, oyh_s.at[0, 0, 0], oyh_r.at[0, 0, 0], other_yh).start()
 
     def out_last(o, out):
         @pl.when(holder)
         def _():
             total = at_home(o, yh)
             if o == 0:
-                arrived(oyh_0, oyh_s.at[0, 0], oyh_r.at[0, 0])
+                arrived(oyh_0, oyh_s.at[0, 0, 0], oyh_r.at[0, 0, 0])
                 total += oyh_0[...].astype(F32)
             outs[o, home] = total.astype(BF16)
             remote(outs.at[o, home, 1 - yl], oyl.at[o], oyl_s.at[o], oyl_r.at[o], other_yl).start()
@@ -448,38 +533,52 @@
             arrived(oyl.at[o], oyl_s.at[o], oyl_r.at[o])
             out[...] = oyl[o]
 
-    grad_send(2, 0, 1)
-    out_partial(0, 1)
-    out_partial(0, 0)
-    grad_send(2, 1)
-    layer_out_to_homes()
+    unpack(2)
+    activate(0)
+    out_partial(0, 1, 0)
+    out_partial(0, 0, 0)
+    tokens_from_core(1, 0)
+    exchange(2, 0)
+    tokens_from_core(1, 1)
+    exchange(2, 1)
+    layer_out_leaves(0)
+    activate(1)
+    out_partial(0, 1, 1)
+    out_partial(0, 0, 1)
+    relays(0, 0)
+    grad_send(2, 0, 2)
+    layer_out_leaves(1)
+    grad_send(2, 2)
     grad_transit(2)
-    exchanged(2)
-
-    def delta(i):
-        h, rows = i // 4, pl.ds(pl.multiple_of((i % 4) * 64, 64), 64)
-        hg = pre[2, h, rows, :] + precv[2, h, rows, :].astype(F32)
-        deltas[0, h, rows, :] = (hg * act[0, h, rows, :]).astype(BF16)
-        deltas[1, h, rows, :] = (hg * act[1, h, rows, :]).astype(BF16)
-
-    loop(8, delta)
+    delta(0)
+    out_partial(1, 1, 0)
+    out_partial(1, 0, 0)
+    relays(0, 1)
+    token_grad_to_yh(0)
+    delta(1)
+    out_partial(1, 1, 1)
+    out_partial(1, 0, 1)
     grad_send(0, 0, 1)
-    out_partial(1, 1)
-    out_partial(1, 0)
+    token_grad_to_yh(1)
     grad_send(0, 1, 2)
-    token_grad_to_yh()
-    grad_send(0, 2)
+    grad_send(0, 3, 4)
     grad_send(1, 0, 1)
+    token_grad_leaves(0)
+    grad_send(1, 1, 2)
+    grad_send(1, 3, 4)
+    layer_out_yh()
     grad_transit(0)
-    token_grad_to_homes()
-    grad_send(1, 1)
+    token_grad_leaves(1)
+    relays(1, 0)
     grad_transit(1)
-    layer_out_yh()
+    grad_send(0, 2, 3)
+    grad_send(1, 2, 3)
+    relays(1, 1)
     out_last(0, layer_out)
+    grad_finish(2)
     out_last(1, token_grad)
-    grad_finish(2, down_g)
-    grad_finish(0, gate_g)
-    grad_finish(1, up_g)
+    grad_finish(0)
+    grad_finish(1)
     out_other(0, layer_out)
     out_other(1, token_grad)
 
@@ -501,34 +600,41 @@
 
         @pl.when(jnp.logical_not(jnp.logical_and(holder, (j // 2) % 2 * 4 + yl * 2 + j % 2 == z)))
         def _():
-            @pl.when(i % 2 == 0)
+            left(piece, oz_s.at[0, j, i % 2])
+
+            @pl.when(j // 4 == yh)
             def _():
-                left(rows, oz_s.at[0, j])
-
-                @pl.when(j // 4 == yh)
-                def _():
-                    left(rows, oz_s.at[1, j])
+                left(piece, oz_s.at[1, j, i % 2])
 
         for o in range(2):
-
-            @pl.when(i % 2 == o)
-            def _():
-                left(rows, oc_s.at[o, j])
+            left(piece, oc_s.at[o, j, i % 2])
 
     loop(16, tokens_left)
 
+    for tc, w in ((0, 0), (1, 0), (1, 1)):
+        for e in range(1 - tc, 2):
+            for d in range(2):
+                for hop in range(1, 4 if e == d else 3):
+                    at_z = (z + (NZ - hop if d == 0 else hop)) % NZ
+
+                    @pl.when(holds(at_z))
+                    def _():
+                        left(piece, zf_s.at[tc, chunk((yh + w) % 2, at_z, c) // 2, e])
+
     def z_left(k):
-        for e in range(2):
-            for tc, w in ((0, 0), (1, 0), (1, 1)):
-                left(piece, z_s.at[tc, w, e, k])
+        for tc, w, e in ((0, 0, 1), (1, 0, 0), (1, 0, 1), (1, 1, 0), (1, 1, 1)):
+            left(piece, z_s.at[tc, w, e, k])
 
     for i in range(4):
-        left(rows, oyh_s.at[1, i])
+        for h in range(2):
+            left(piece, oyh_s.at[1, i, h])
 
     @pl.when(holder)
     def _():
-        loop(7, z_left)
-        left(rows, oyh_s.at[0, 0])
+        loop(2, z_left)
+        for k in range(7):
+            left(piece, zd_s.at[k])
+        left(rows, oyh_s.at[0, 0, 0])
         for o in range(2):
             left(piece, yh_s.at[1, place(z), o])
             left(piece, oyl_s.at[o])
@@ -551,15 +657,29 @@
             left(psend.at[0, 0], p_s.at[m, h])
 
 
+def finish(out, grad, gown, gate_m, up_m, down_m, layer_out, token_grad, gate_g, up_g, down_g):
+    layer_out[...] = out[...]
+    token_grad[...] = grad[...]
+    for m, (mask, dst) in enumerate(((gate_m, gate_g), (up_m, up_g), (down_m, down_g))):
+        count = jnp.int32(0)
+        for t in range(TILES):
+            r, k = t // 4, t % 4
+            kept = mask[r, k] > 0
+            dst[r * BLK:(r + 1) * BLK, k * BLK:(k + 1) * BLK] = gown[m, jnp.where(kept, count, SLOTS)]
+            count = count + jnp.where(kept, 1, 0)
+
+
 def body(tokens, cotangent, gate_weight, up_weight, down_weight, gate_mask, up_mask, down_mask):
     vmem, smem = pl.BlockSpec(memory_space=pltpu.VMEM), pl.BlockSpec(memory_space=pltpu.SMEM)
     dma = pltpu.SemaphoreType.DMA
     shapes = (tokens, cotangent, gate_weight, up_weight, down_weight)
-    return pl.pallas_call(
+    shapes = tuple(jax.ShapeDtypeStruct(a.shape, a.dtype) for a in shapes)
+    masks = (gate_mask, up_mask, down_mask)
+    sums = pl.pallas_call(
         kernel,
-        out_shape=tuple(jax.ShapeDtypeStruct(a.shape, a.dtype) for a in shapes),
+        out_shape=(*shapes[:2], jax.ShapeDtypeStruct((3, SLOTS + 1, BLK, BLK), BF16)),
         in_specs=[vmem] * 5 + [smem] * 3,
-        out_specs=(vmem,) * 5,
+        out_specs=(vmem,) * 3,
         scratch_shapes=[
             pltpu.VMEM((2, 16, 2, 256, BLK), BF16),
             *[pltpu.VMEM((NX, SLOTS + 1, BLK, BLK), BF16)] * 3,
@@ -577,30 +697,33 @@
             pltpu.VMEM((NX, 3, SLOTS, BLK, BLK), BF16),
             pltpu.VMEM((2, 3, 4, BLK, BLK), BF16),
             pltpu.VMEM((2, 3, SLOTS, BLK, BLK), BF16),
-            pltpu.VMEM((3, SLOTS + 1, BLK, BLK), BF16),
             pltpu.VMEM((2, 16, 2, 256, BLK), BF16),
             pltpu.VMEM((2, 8, 2, 256, BLK), BF16),
-            pltpu.VMEM((2, NZ, 2, 256, BLK), BF16),
-            pltpu.VMEM((NZ, 2, 256, BLK), BF16),
+            pltpu.VMEM((2, 4, 2, 256, BLK), BF16),
+            pltpu.VMEM((4, 2, 256, BLK), BF16),
+            pltpu.VMEM((2, 8, 2, 256, BLK), BF16),
             pltpu.VMEM((2, 256, BLK), BF16),
             pltpu.VMEM((4, 2, 256, BLK), BF16),
             pltpu.VMEM((2, 256, BLK), BF16),
             dma((2,)), dma((2,)), dma((2, 4, 2)), dma((2, 4, 2)),
-            dma((2, 2, 2, 7)), dma((2, 8, 2)),
+            dma((2, 2, 2, 2)), dma((2, 8, 2)), dma((2, 8, 2)), dma((7,)),
             dma((2, 8, 2)), dma((2, 8, 2)),
             dma((2, 3, 2)), dma((3, 2)), dma((3, 3, 2)),
             dma((3,)), dma((3,)), dma(()),
             dma((3, 2)), dma((3, 2)),
             dma((2, 3)), dma((2, 3)), dma((2, 3, 2)), dma((2, 3, 2)),
-            dma((2, 8)), dma((2, 8)),
-            dma((2, 8)), dma((2, 2, NZ)),
-            dma((2, 4)), dma((2, 4)), dma((2,)), dma((2,)),
+            dma((2, 8, 2)), dma((2, 8, 2)),
+            dma((2, 8, 2)), dma((2, 2, 4, 2)), dma((2, 8, 2)),
+            dma((2, 4, 2)), dma((2, 4, 2)), dma((2,)), dma((2,)),
         ],
         compiler_params=pltpu.CompilerParams(
             collective_id=0, has_side_effects=True, vmem_limit_bytes=58 * 2**20
         ),
         cost_estimate=pl.CostEstimate(flops=9_663_676_416, bytes_accessed=4 * 2**20, transcendentals=262144),
-    )(tokens, cotangent, gate_weight, up_weight, down_weight, gate_mask, up_mask, down_mask)
+    )(*(tokens, cotangent, gate_weight, up_weight, down_weight), *masks)
+    return pl.pallas_call(
+        finish, out_shape=shapes, in_specs=[vmem] * 3 + [smem] * 3, out_specs=(vmem,) * 5
+    )(*sums, *masks)
 
 
 def solution(mesh):

time: 146 us -> 113 us (0.77)
  Pallas kernels: 138 us -> 112 us
  local copies, waits for them, and re-layouts: 6.09 us -> 0 us
    pallas_call x1 -> x2, Pallas kernels: 138 us -> 112 us  [the longest x1 109 us: body(): pl.pallas_call(kernel, out_shape=(*shapes[:2], jax.ShapeDtypeStruct((3, S...]
    unnamed x11 -> x0, local copies, waits for them, and re-layouts: 6.09 us -> none
where the time goes in v4:
time: 113 us; the launch traced here: 112 us
  Pallas kernels  112 us (99%)
    pallas_call x1, Pallas kernels, body(): pl.pallas_call(kernel, out_shape=(*shapes[:2], jax.ShapeDtypeStruct((3, S...  109 us
    pallas_call x1, Pallas kernels, body(): pl.pallas_call(finish, out_shape=shapes, in_specs=[vmem] * 3 + [smem] * 3...  2.81 us

profile of v4, /device:TPU:8, one launch (start us, length us, event | category | flops | bytes accessed | tf_op | source)
XLA Modules:
  0.0 112.3 jit_solution(944874693768748890)
XLA Ops:
  0.6 108.8 %shard_map.119 = (bf16[256,128]{1,0:T(8,128)(2,1)}, bf16[256,128]{1,0:T(8,128)(2,1)}, bf16[3,9,128,128]{3,2,1,0:T(8,128)(2,1)}) custom-call(bf16[256,128]{1,0:T(8,128)(2,1)} %tok.1, bf16[256,128]{1,0:T(8,128)(2,1)} %cot.1, bf16[512,512]{1,0:T(8,128)(2,1)} %gate_w.1, bf16[512,512]{1,0:T(8,128)(2,1)} %up_w.1, bf16[512,512]{1,0:T(8,128)(2,1)} %down_w.1, ...), custom_call_target="tpu_custom_call" | custom-call | flops 9663676416 | bytes 4194304 | tf_op jit(solution)/shard_map/pallas_call | solution.py:678
  109.4 2.8 %shard_map.120 = (bf16[256,128]{1,0:T(8,128)(2,1)}, bf16[256,128]{1,0:T(8,128)(2,1)}, bf16[512,512]{1,0:T(8,128)(2,1)}, bf16[512,512]{1,0:T(8,128)(2,1)}, bf16[512,512]{1,0:T(8,128)(2,1)}) custom-call(bf16[256,128]{1,0:T(8,128)(2,1)} %get-tuple-element.8.out, bf16[256,128]{1,0:T(8,128)(2,1)} %get-tuple-element.9.grad, ...), custom_call_target="tpu_custom_call" | custom-call | tf_op jit(solution)/shard_map/pallas_call | solution.py:724

commit v5 on v4

--- a/solution.py
+++ b/solution.py
@@ -545,19 +545,19 @@
     activate(1)
     out_partial(0, 1, 1)
     out_partial(0, 0, 1)
+    grad_send(2, 0, 2)
     relays(0, 0)
-    grad_send(2, 0, 2)
     layer_out_leaves(1)
     grad_send(2, 2)
     grad_transit(2)
     delta(0)
     out_partial(1, 1, 0)
     out_partial(1, 0, 0)
-    relays(0, 1)
     token_grad_to_yh(0)
     delta(1)
     out_partial(1, 1, 1)
     out_partial(1, 0, 1)
+    relays(0, 1)
     grad_send(0, 0, 1)
     token_grad_to_yh(1)
     grad_send(0, 1, 2)

time: 113 us -> 111 us (0.982)
  Pallas kernels: 112 us -> 110 us
    pallas_call x1, Pallas kernels: 109 us -> 107 us  [body(): pl.pallas_call(kernel, out_shape=(*shapes[:2], jax.ShapeDtypeStruct((3, S...]
where the time goes in v5:
time: 111 us
  Pallas kernels  110 us (99%)
    pallas_call x1, Pallas kernels, body(): pl.pallas_call(kernel, out_shape=(*shapes[:2], jax.ShapeDtypeStruct((3, S...  107 us
    pallas_call x1, Pallas kernels, body(): pl.pallas_call(finish, out_shape=shapes, in_specs=[vmem] * 3 + [smem] * 3...  2.81 us

profile of v5, /device:TPU:8, one launch (start us, length us, event | category | flops | bytes accessed | tf_op | source)
XLA Modules:
  0.0 110.7 jit_solution(10774536737780108957)
XLA Ops:
  0.6 107.3 %shard_map.119 = (bf16[256,128]{1,0:T(8,128)(2,1)}, bf16[256,128]{1,0:T(8,128)(2,1)}, bf16[3,9,128,128]{3,2,1,0:T(8,128)(2,1)}) custom-call(bf16[256,128]{1,0:T(8,128)(2,1)} %tok.1, bf16[256,128]{1,0:T(8,128)(2,1)} %cot.1, bf16[512,512]{1,0:T(8,128)(2,1)} %gate_w.1, bf16[512,512]{1,0:T(8,128)(2,1)} %up_w.1, bf16[512,512]{1,0:T(8,128)(2,1)} %down_w.1, ...), custom_call_target="tpu_custom_call" | custom-call | flops 9663676416 | bytes 4194304 | tf_op jit(solution)/shard_map/pallas_call | solution.py:678
  107.9 2.8 %shard_map.120 = (bf16[256,128]{1,0:T(8,128)(2,1)}, bf16[256,128]{1,0:T(8,128)(2,1)}, bf16[512,512]{1,0:T(8,128)(2,1)}, bf16[512,512]{1,0:T(8,128)(2,1)}, bf16[512,512]{1,0:T(8,128)(2,1)}) custom-call(bf16[256,128]{1,0:T(8,128)(2,1)} %get-tuple-element.8.out, bf16[256,128]{1,0:T(8,128)(2,1)} %get-tuple-element.9.grad, ...), custom_call_target="tpu_custom_call" | custom-call | tf_op jit(solution)/shard_map/pallas_call | solution.py:724

commit v6 on v5

--- a/solution.py
+++ b/solution.py
@@ -563,15 +563,15 @@
     grad_send(0, 1, 2)
     grad_send(0, 3, 4)
     grad_send(1, 0, 1)
+    grad_transit(0)
     token_grad_leaves(0)
     grad_send(1, 1, 2)
     grad_send(1, 3, 4)
+    token_grad_leaves(1)
     layer_out_yh()
-    grad_transit(0)
-    token_grad_leaves(1)
+    grad_send(0, 2, 3)
     relays(1, 0)
     grad_transit(1)
-    grad_send(0, 2, 3)
     grad_send(1, 2, 3)
     relays(1, 1)
     out_last(0, layer_out)

time: 111 us -> 111 us (level)
  no operation moved by 1% of the time
where the time goes in v6:
time: 111 us
  Pallas kernels  111 us (100%)
    pallas_call x1, Pallas kernels, body(): pl.pallas_call(kernel, out_shape=(*shapes[:2], jax.ShapeDtypeStruct((3, S...  108 us
    pallas_call x1, Pallas kernels, body(): pl.pallas_call(finish, out_shape=shapes, in_specs=[vmem] * 3 + [smem] * 3...  2.81 us

profile of v6, /device:TPU:8, one launch (start us, length us, event | category | flops | bytes accessed | tf_op | source)
XLA Modules:
  0.0 111.2 jit_solution(7696306995561788758)
XLA Ops:
  0.6 107.7 %shard_map.119 = (bf16[256,128]{1,0:T(8,128)(2,1)}, bf16[256,128]{1,0:T(8,128)(2,1)}, bf16[3,9,128,128]{3,2,1,0:T(8,128)(2,1)}) custom-call(bf16[256,128]{1,0:T(8,128)(2,1)} %tok.1, bf16[256,128]{1,0:T(8,128)(2,1)} %cot.1, bf16[512,512]{1,0:T(8,128)(2,1)} %gate_w.1, bf16[512,512]{1,0:T(8,128)(2,1)} %up_w.1, bf16[512,512]{1,0:T(8,128)(2,1)} %down_w.1, ...), custom_call_target="tpu_custom_call" | custom-call | flops 9663676416 | bytes 4194304 | tf_op jit(solution)/shard_map/pallas_call | solution.py:678
  108.4 2.8 %shard_map.120 = (bf16[256,128]{1,0:T(8,128)(2,1)}, bf16[256,128]{1,0:T(8,128)(2,1)}, bf16[512,512]{1,0:T(8,128)(2,1)}, bf16[512,512]{1,0:T(8,128)(2,1)}, bf16[512,512]{1,0:T(8,128)(2,1)}) custom-call(bf16[256,128]{1,0:T(8,128)(2,1)} %get-tuple-element.8.out, bf16[256,128]{1,0:T(8,128)(2,1)} %get-tuple-element.9.grad, ...), custom_call_target="tpu_custom_call" | custom-call | tf_op jit(solution)/shard_map/pallas_call | solution.py:724
